TPU v7x, 32 devices: a whole 2x2x4 slice. The times are simulated.
32 devices in a mesh: space: 4 (over z), tp: 8 (over y, x, core).
Axes of the slice: x: 2, y: 2, z: 4, core: 2. Of those that a mesh axis runs over, the one named last changes fastest.
Arguments:
- queries: bfloat16 [32, 32, 4, 1024], P('space', 'tp'), may hold values from -9.7 to 9.7
- key_field: bfloat16 [32, 32, 4, 1024], P('space', 'tp'), may hold values from -4 to 4
- value_field: bfloat16 [32, 32, 4, 1024], P('space', 'tp'), may hold values from -12 to 12
- upstream: bfloat16 [32, 32, 4, 1024], P('space', 'tp'), may hold values from -6 to 6
Outputs:
- out: bfloat16 [32, 32, 4, 1024], P('space', 'tp')
- grad_queries: bfloat16 [32, 32, 4, 1024], P('space', 'tp')
- grad_keys: bfloat16 [32, 32, 4, 1024], P('space', 'tp')
- grad_values: bfloat16 [32, 32, 4, 1024], P('space', 'tp')
All inputs are finite; a program needn't handle non-finite values.
Results may differ from a plain program's by a relative error of at most 0.0093.
Values may be sent and summed in bfloat16 or wider, within the bound.
A program may use at most 64 MiB of HBM per device.

v0:
```python
import math

import jax
import jax.numpy as jnp
from jax import lax
from jax.sharding import PartitionSpec as P

HEADS = 16
RADIUS = 3


blocked_score = -1e30
heads_group = 4


def padded(cells, sides, width):
    for axis, dim in sides:
        count = lax.axis_size(axis)
        ends = count - 1
        head = lax.slice_in_dim(cells, 0, width, axis=dim)
        tail = lax.slice_in_dim(cells, cells.shape[dim] - width, cells.shape[dim], axis=dim)
        cells = jnp.concatenate(
            [
                lax.ppermute(tail, axis, [(i, (i + 1) % count) for i in range(ends)]),
                cells,
                lax.ppermute(head, axis, [((i + 1) % count, i) for i in range(ends)]),
            ],
            axis=dim,
        )
    return cells


def from_behind(x, axis, by):
    peers = lax.axis_size(axis)
    pairs = [(i, i + by) for i in range(peers) if 0 <= i + by < peers]
    return lax.ppermute(x, axis, pairs)


def window_mask(along_x, along_y, depth_z, first_x, first_y, grid_x, grid_y, rim_width):
    centre_x, centre_y, centre_z = jnp.meshgrid(
        jnp.arange(along_x, dtype=jnp.int32),
        jnp.arange(along_y, dtype=jnp.int32),
        jnp.arange(depth_z, dtype=jnp.int32),
        indexing="ij",
    )
    other_x, other_y, other_z = jnp.meshgrid(
        jnp.arange(along_x + 2 * rim_width, dtype=jnp.int32),
        jnp.arange(along_y + 2 * rim_width, dtype=jnp.int32),
        jnp.arange(depth_z, dtype=jnp.int32),
        indexing="ij",
    )
    centre_x = centre_x.reshape(-1)[:, None]
    centre_y = centre_y.reshape(-1)[:, None]
    centre_z = centre_z.reshape(-1)[:, None]
    other_x = other_x.reshape(-1)[None, :]
    other_y = other_y.reshape(-1)[None, :]
    other_z = other_z.reshape(-1)[None, :]
    within = (
        (jnp.abs(other_x - centre_x - rim_width) <= rim_width)
        & (jnp.abs(other_y - centre_y - rim_width) <= rim_width)
        & (jnp.abs(other_z - centre_z) <= rim_width)
    )
    global_x = first_x + other_x - rim_width
    global_y = first_y + other_y - rim_width
    inside = (global_x >= 0) & (global_x < grid_x) & (global_y >= 0) & (global_y < grid_y)
    return within & inside


def take_heads(matrix, group_index, group_width):
    part = lax.dynamic_slice_in_dim(matrix, group_index * group_width, group_width, 1)
    return part.reshape(matrix.shape[0], heads_group, -1)


def take_stats(matrix, group_index):
    return jnp.transpose(
        lax.dynamic_slice_in_dim(matrix, group_index * heads_group, heads_group, 1)
    )


def regroup(stacked):
    groups, row_total, group_width = stacked.shape
    return jnp.transpose(stacked, (1, 0, 2)).reshape(row_total, groups * group_width)


def regroup_heads(stacked):
    groups, per_group, row_total = stacked.shape
    return jnp.transpose(stacked, (2, 0, 1)).reshape(row_total, groups * per_group)


def attend_forward(centre_q, other_k, other_v, allowed, head_size):
    row_total = centre_q.shape[0]
    group_width = heads_group * head_size
    inv_root = 1.0 / math.sqrt(head_size)

    def one_group(group_index):
        query_part = take_heads(centre_q, group_index, group_width)
        key_part = take_heads(other_k, group_index, group_width)
        value_part = take_heads(other_v, group_index, group_width)
        scores = (
            jnp.einsum("qhd,khd->hqk", query_part, key_part, preferred_element_type=jnp.float32)
            * inv_root
        )
        scores = jnp.where(allowed[None], scores, blocked_score)
        highest = jnp.max(scores, axis=2, keepdims=True)
        summed = jnp.sum(jnp.exp(scores - highest), axis=2, keepdims=True)
        log_total = highest + jnp.log(summed)
        weights = jnp.exp(scores - log_total).astype(jnp.bfloat16)
        attended = jnp.einsum(
            "hqk,khd->qhd", weights, value_part, preferred_element_type=jnp.float32
        ).astype(jnp.bfloat16)
        return (attended.reshape(row_total, group_width), log_total[:, :, 0])

    attended, log_total = lax.map(one_group, jnp.arange(HEADS // heads_group, dtype=jnp.int32))
    return (regroup(attended), regroup_heads(log_total))


def attend_queries(
    centre_q, centre_up, centre_lse, centre_dots, other_k, other_v, allowed, head_size
):
    row_total = centre_q.shape[0]
    other_total = other_k.shape[0]
    group_width = heads_group * head_size
    inv_root = 1.0 / math.sqrt(head_size)

    def one_group(group_index):
        up_part = take_heads(centre_up, group_index, group_width)
        query_part = take_heads(centre_q, group_index, group_width)
        key_part = take_heads(other_k, group_index, group_width)
        value_part = take_heads(other_v, group_index, group_width)
        lse_part = take_stats(centre_lse, group_index)
        dot_part = take_stats(centre_dots, group_index)
        scores = (
            jnp.einsum("qhd,khd->hqk", query_part, key_part, preferred_element_type=jnp.float32)
            * inv_root
        )
        scores = jnp.where(allowed[None], scores, blocked_score)
        exact_prob = jnp.exp(scores - lse_part[:, :, None])
        d_prob = jnp.einsum("qhd,khd->hqk", up_part, value_part, preferred_element_type=jnp.float32)
        dscore = (exact_prob * (d_prob - dot_part[:, :, None])).astype(jnp.bfloat16)
        grad_q = (
            jnp.einsum("hqk,khd->qhd", dscore, key_part, preferred_element_type=jnp.float32)
            * inv_root
        ).astype(jnp.bfloat16)
        weights = exact_prob.astype(jnp.bfloat16)
        part_k = (
            jnp.einsum("hqk,qhd->khd", dscore, query_part, preferred_element_type=jnp.float32)
            * inv_root
        )
        part_v = jnp.einsum("hqk,qhd->khd", weights, up_part, preferred_element_type=jnp.float32)
        return (
            grad_q.reshape(row_total, group_width),
            part_k.reshape(other_total, group_width),
            part_v.reshape(other_total, group_width),
        )

    results = lax.map(one_group, jnp.arange(HEADS // heads_group, dtype=jnp.int32))
    return tuple((regroup(stacked) for stacked in results))


def head_products(flat_up, attended, head_count):
    fixed = lax.optimization_barrier(attended).astype(jnp.float32)
    product = flat_up.astype(jnp.float32) * fixed
    return product.reshape(product.shape[0], head_count, -1).sum(axis=2)


def fold_rims(pieces, axis_dim, rim_width, sender):
    extent = pieces.shape[axis_dim]
    interior = extent - 2 * rim_width
    low_rim = lax.slice_in_dim(pieces, 0, rim_width, axis=axis_dim)
    high_rim = lax.slice_in_dim(pieces, extent - rim_width, extent, axis=axis_dim)
    centre_part = lax.slice_in_dim(pieces, rim_width, extent - rim_width, axis=axis_dim)
    from_next = sender(low_rim, -1)
    from_prev = sender(high_rim, 1)
    padding_low = [(0, 0)] * pieces.ndim
    padding_high = [(0, 0)] * pieces.ndim
    padding_low[axis_dim] = (0, interior - rim_width)
    padding_high[axis_dim] = (interior - rim_width, 0)
    return centre_part + jnp.pad(from_prev, padding_low) + jnp.pad(from_next, padding_high)


def on_device(queries, key_field, value_field, upstream):
    along_x, along_y, depth_z, features = queries.shape
    head_size = features // HEADS
    row_total = along_x * along_y * depth_z
    span_x = along_x + 2 * RADIUS
    span_y = along_y + 2 * RADIUS
    others = span_x * span_y * depth_z
    allowed = window_mask(
        along_x,
        along_y,
        depth_z,
        lax.axis_index("space") * along_x,
        lax.axis_index("tp") * along_y,
        along_x * lax.axis_size("space"),
        along_y * lax.axis_size("tp"),
        RADIUS,
    )
    key_rims = padded(jnp.stack([key_field, value_field]), (("space", 1), ("tp", 2)), RADIUS)
    other_k = key_rims[0].reshape(others, features)
    other_v = key_rims[1].reshape(others, features)
    flat_q = queries.reshape(row_total, features)
    flat_up = upstream.reshape(row_total, features)
    attended, log_total = attend_forward(flat_q, other_k, other_v, allowed, head_size)
    dot_terms = head_products(flat_up, attended, HEADS)
    grad_q, part_k, part_v = attend_queries(
        flat_q, flat_up, log_total, dot_terms, other_k, other_v, allowed, head_size
    )
    pieces = jnp.stack([part_k, part_v]).reshape(2, span_x, span_y, depth_z, features)

    def send_space(block_part, offset):
        return from_behind(block_part.astype(jnp.bfloat16), "space", offset).astype(
            block_part.dtype
        )

    def send_tp(block_part, offset):
        return from_behind(block_part, "tp", offset)

    pieces = fold_rims(pieces, 1, RADIUS, send_space)
    pieces = fold_rims(pieces, 2, RADIUS, send_tp)
    grad_k = pieces[0].astype(jnp.bfloat16)
    grad_v = pieces[1].astype(jnp.bfloat16)
    shape_out = (along_x, along_y, depth_z, features)
    return (attended.reshape(shape_out), grad_q.reshape(shape_out), grad_k, grad_v)


def solution(mesh):
    in_specs = (
        P("space", "tp", None, None),
        P("space", "tp", None, None),
        P("space", "tp", None, None),
        P("space", "tp", None, None),
    )
    out_specs = (
        P("space", "tp", None, None),
        P("space", "tp", None, None),
        P("space", "tp", None, None),
        P("space", "tp", None, None),
    )
    return jax.shard_map(
        on_device, mesh=mesh, in_specs=in_specs, out_specs=out_specs, check_vma=False
    )
```

profile of v0, /device:TPU:1, one launch (start us, length us, event | category | flops | bytes accessed | tf_op | source)
XLA Modules:
  0.0 175.9 jit_solution(8167110803918692477)
XLA Ops:
  2.0 4.0 %collective-permute-start = (bf16[2,3,4,4,1024]{4,3,2,1,0:T(4,128)(2,1)S(1)}, bf16[2,3,4,4,1024]{4,3,2,1,0:T(4,128)(2,1)S(1)}, u32[]{:S(2)}, u32[]{:S(2)}) collective-permute-start(bf16[2,3,4,4,1024]{4,3,2,1,0:T(4,128)(2,1)S(1)} %get-tuple-element.344), channel_id=1, source_target_pairs={{0,8},{8,16},{16,24},{1,9},{9,17},{17,25},{2,10},{10,18},{18,26},{... | collective-permute-start | bytes 589832 | tf_op jit(solution)/shard_map/ppermute | solution.py:24
  6.0 1.4 collective-permute-start.1
  7.5 2.1 %collective-permute-done = bf16[2,3,4,4,1024]{4,3,2,1,0:T(4,128)(2,1)S(1)} collective-permute-done((bf16[2,3,4,4,1024]{4,3,2,1,0:T(4,128)(2,1)S(1)}, bf16[2,3,4,4,1024]{4,3,2,1,0:T(4,128)(2,1)S(1)}, u32[]{:S(2)}, u32[]{:S(2)}) %collective-permute-start) | collective-permute-done | bytes 196640 | tf_op jit(solution)/shard_map/ppermute | solution.py:24
  9.6 3.9 %collective-permute-done.1 = bf16[2,3,4,4,1024]{4,3,2,1,0:T(4,128)(2,1)S(1)} collective-permute-done((bf16[2,3,4,4,1024]{4,3,2,1,0:T(4,128)(2,1)S(1)}, bf16[2,3,4,4,1024]{4,3,2,1,0:T(4,128)(2,1)S(1)}, u32[]{:S(2)}, u32[]{:S(2)}) %collective-permute-start.1) | collective-permute-done | bytes 196640 | tf_op jit(solution)/shard_map/ppermute | solution.py:26
  13.5 1.8 %pad_maximum_fusion.1 = bf16[2,14,4,4,1024]{4,3,2,1,0:T(4,128)(2,1)S(1)} fusion(bf16[2,3,4,4,1024]{4,3,2,1,0:T(4,128)(2,1)S(1)} %collective-permute-done.1, bf16[1,8,4,4,1024]{4,3,2,1,0:T(4,128)(2,1)} %bitcast.132, bf16[1,8,4,4,1024]{4,3,2,1,0:T(4,128)(2,1)} %bitcast.135, bf16[2,3,4,4,1024]{4,3,2,1,0:T(4,128)(2,1)S(1)} %collective-permute-done), kind=kLoop, calls=%fused_computation.55 | loop fusion | flops 1376256 | bytes 1835008 | tf_op jit(solution)/shard_map/concatenate | solution.py:22
  16.8 4.9 %collective-permute-start.2 = (bf16[2,14,3,4,1024]{4,3,2,1,0:T(4,128)(2,1)}, bf16[2,14,3,4,1024]{4,3,2,1,0:T(4,128)(2,1)S(1)}, u32[]{:S(2)}, u32[]{:S(2)}) collective-permute-start(bf16[2,14,3,4,1024]{4,3,2,1,0:T(4,128)(2,1)} %get-tuple-element.340), channel_id=1, source_target_pairs={{0,1},{1,2},{2,3},{3,4},{4,5},{5,6},{6,7},{8,9},{9,10},{10,11},{11... | collective-permute-start | bytes 2064392 | tf_op jit(solution)/shard_map/ppermute | solution.py:24
  21.6 1.9 %collective-permute-start.3 = (bf16[2,14,3,4,1024]{4,3,2,1,0:T(4,128)(2,1)S(1)}, bf16[2,14,3,4,1024]{4,3,2,1,0:T(4,128)(2,1)}, u32[]{:S(2)}, u32[]{:S(2)}) collective-permute-start(bf16[2,14,3,4,1024]{4,3,2,1,0:T(4,128)(2,1)S(1)} %get-tuple-element.341), channel_id=1, source_target_pairs={{1,0},{2,1},{3,2},{4,3},{5,4},{6,5},{7,6},{9,8},{10,9},{11,10},{12... | collective-permute-start | bytes 2064392 | tf_op jit(solution)/shard_map/ppermute | solution.py:26
  25.7 4.1 %collective-permute-done.2 = bf16[2,14,3,4,1024]{4,3,2,1,0:T(4,128)(2,1)S(1)} collective-permute-done((bf16[2,14,3,4,1024]{4,3,2,1,0:T(4,128)(2,1)}, bf16[2,14,3,4,1024]{4,3,2,1,0:T(4,128)(2,1)S(1)}, u32[]{:S(2)}, u32[]{:S(2)}) %collective-permute-start.2) | collective-permute-done | bytes 688160 | tf_op jit(solution)/shard_map/ppermute | solution.py:24
  30.7 8.2 %collective-permute-done.3 = bf16[2,14,3,4,1024]{4,3,2,1,0:T(4,128)(2,1)} collective-permute-done((bf16[2,14,3,4,1024]{4,3,2,1,0:T(4,128)(2,1)S(1)}, bf16[2,14,3,4,1024]{4,3,2,1,0:T(4,128)(2,1)}, u32[]{:S(2)}, u32[]{:S(2)}) %collective-permute-start.3) | collective-permute-done | bytes 688160 | tf_op jit(solution)/shard_map/ppermute | solution.py:26
  38.8 3.2 %pad_maximum_fusion = bf16[2,14,10,4,1024]{4,3,2,1,0:T(4,128)(2,1)S(1)} fusion(bf16[2,14,3,4,1024]{4,3,2,1,0:T(4,128)(2,1)} %collective-permute-done.3, bf16[2,3,4,4,1024]{4,3,2,1,0:T(4,128)(2,1)} %copy-done.5, bf16[1,8,4,4,1024]{4,3,2,1,0:T(4,128)(2,1)S(1)} %bitcast.133, bf16[1,8,4,4,1024]{4,3,2,1,0:T(4,128)(2,1)S(1)} %bitcast.136, ...), kind=kLoop, calls=%fused_computation.51 | loop fusion | flops 5734400 | bytes 4587520 | tf_op jit(solution)/shard_map/concatenate | solution.py:22
  42.0 2.4 %fusion.28 = (bf16[1,14,10,4,1024]{4,3,2,1,0:T(4,128)(2,1)}, bf16[1,14,10,4,1024]{4,3,2,1,0:T(4,128)(2,1)}) fusion(bf16[2,14,10,4,1024]{4,3,2,1,0:T(4,128)(2,1)S(1)} %pad_maximum_fusion), kind=kLoop, calls=%fused_computation.70 | loop fusion | bytes 4587520 | tf_op jit(solution)/shard_map/slice | solution.py:199
  44.4 3.2 %reshape_squeeze.7 = bf16[560,1024]{1,0:T(8,128)(2,1)} reshape(bf16[1,14,10,4,1024]{4,3,2,1,0:T(4,128)(2,1)} %get-tuple-element.338) | data formatting | bytes 2293760 | tf_op jit(solution)/shard_map/reshape;squeeze | solution.py:199
  47.6 1.7 copy.30
  50.5 1.7 copy.28
  52.2 16.5 %while.28 = (s32[]{:T(128)}, bf16[4,128,256]{1,2,0:T(8,128)(2,1)S(1)}, f32[4,4,128]{2,1,0:T(4,128)}, s32[4]{0:T(128)S(1)}, bf16[560,1024]{0,1:T(8,128)(2,1)S(1)}...) while((s32[]{:T(128)}, ...), condition=%wide.region_3.4_spmd.clone, body=%wide.region_0.3_spmd.clone.sunk | while | flops 76443136 | bytes 5722983 | solution.py:113
  69.6 1.8 %convert_multiply_fusion = f32[128,1024]{1,0:T(8,128)} fusion(bf16[128,1024]{1,0:T(8,128)(2,1)} %copy.41, bf16[128,1024]{1,0:T(8,128)(2,1)S(1)} %reshape.135), kind=kLoop, calls=%fused_computation.57 | loop fusion | flops 393216 | bytes 1048576 | tf_op jit(solution)/shard_map/mul | solution.py:162
  71.4 2.1 %copy.33 = f32[128,1024]{0,1:T(8,128)} copy(f32[128,1024]{1,0:T(8,128)} %convert_multiply_fusion) | data formatting | bytes 1048576 | tf_op jit(solution)/shard_map/mul | solution.py:162
  75.3 36.9 %while.29 = (s32[]{:T(128)}, bf16[4,128,256]{1,2,0:T(8,128)(2,1)}, f32[4,560,256]{1,2,0:T(8,128)}, f32[4,560,256]{1,2,0:T(8,128)}, s32[4]{0:T(128)S(1)}, /*index...) while((s32[]{:T(128)}, bf16[4,128,256]{1,2,0:T(8,128)(2,1)}, ...), condition=%wide.region_6.7_spmd.clone, body=%wide.region_5.6_spmd.clone.sunk | while | flops 186720256 | bytes 11863733 | solution.py:156
  78.7 1.4 fusion.80
  112.2 4.0 %copy.40 = f32[560,4,256]{2,1,0:T(4,128)} copy(f32[560,4,256]{0,2,1:T(8,128)} %bitcast.129) | data formatting | bytes 4587520 | tf_op jit(solution)/shard_map/transpose | solution.py:82
  116.2 3.1 %stack.20 = f32[1,14,10,4,1024]{4,3,2,1,0:T(4,128)S(1)} reshape(f32[560,4,256]{2,1,0:T(4,128)} %copy.40) | data formatting | bytes 4587520 | tf_op jit(solution)/shard_map/stack | solution.py:208
  119.3 4.0 %copy.39 = f32[560,4,256]{2,1,0:T(4,128)} copy(f32[560,4,256]{0,2,1:T(8,128)} %bitcast.130) | data formatting | bytes 4587520 | tf_op jit(solution)/shard_map/transpose | solution.py:82
  123.3 3.9 %stack.19 = f32[1,14,10,4,1024]{4,3,2,1,0:T(4,128)} reshape(f32[560,4,256]{2,1,0:T(4,128)} %copy.39) | data formatting | bytes 4587520 | tf_op jit(solution)/shard_map/stack | solution.py:208
  127.3 2.1 %constant_dynamic-update-slice_fusion.5 = f32[2,14,10,4,1024]{4,3,2,1,0:T(4,128)S(1)} fusion(f32[1,14,10,4,1024]{4,3,2,1,0:T(4,128)} %stack.19), kind=kLoop, calls=%fused_computation.63 | loop fusion | bytes 4587520
  131.7 3.4 %collective-permute-start.4 = (bf16[2,3,10,4,1024]{4,3,2,1,0:T(4,128)(2,1)S(1)}, bf16[2,3,10,4,1024]{4,3,2,1,0:T(4,128)(2,1)S(1)}, u32[]{:S(2)}, u32[]{:S(2)}) collective-permute-start(bf16[2,3,10,4,1024]{4,3,2,1,0:T(4,128)(2,1)S(1)} %get-tuple-element.336), channel_id=1, source_target_pairs={{0,8},{8,16},{16,24},{1,9},{9,17},{17,25},{2,10},{10,18},{18,26},{... | collective-permute-start | bytes 1474568 | tf_op jit(solution)/shard_map/ppermute | solution.py:36
  136.5 4.4 %collective-permute-done.4 = bf16[2,3,10,4,1024]{4,3,2,1,0:T(4,128)(2,1)S(1)} collective-permute-done((bf16[2,3,10,4,1024]{4,3,2,1,0:T(4,128)(2,1)S(1)}, bf16[2,3,10,4,1024]{4,3,2,1,0:T(4,128)(2,1)S(1)}, u32[]{:S(2)}, u32[]{:S(2)}) %collective-permute-start.4) | collective-permute-done | bytes 491552 | tf_op jit(solution)/shard_map/ppermute | solution.py:36
  140.9 3.8 %collective-permute-done.5 = bf16[2,3,10,4,1024]{4,3,2,1,0:T(4,128)(2,1)S(1)} collective-permute-done((bf16[2,3,10,4,1024]{4,3,2,1,0:T(4,128)(2,1)S(1)}, bf16[2,3,10,4,1024]{4,3,2,1,0:T(4,128)(2,1)S(1)}, u32[]{:S(2)}, u32[]{:S(2)}) %collective-permute-start.5) | collective-permute-done | bytes 491552 | tf_op jit(solution)/shard_map/ppermute | solution.py:36
  147.1 7.8 %collective-permute-start.6 = (f32[2,8,3,4,1024]{4,3,2,1,0:T(4,128)}, f32[2,8,3,4,1024]{4,3,2,1,0:T(4,128)}, u32[]{:S(2)}, u32[]{:S(2)}) collective-permute-start(f32[2,8,3,4,1024]{4,3,2,1,0:T(4,128)} %get-tuple-element.334), channel_id=1, source_target_pairs={{0,1},{1,2},{2,3},{3,4},{4,5},{5,6},{6,7},{8,9},{9,10},{10,11},{11... | collective-permute-start | bytes 2359304 | tf_op jit(solution)/shard_map/ppermute | solution.py:36
  154.8 1.9 %collective-permute-start.7 = (f32[2,8,3,4,1024]{4,3,2,1,0:T(4,128)}, f32[2,8,3,4,1024]{4,3,2,1,0:T(4,128)}, u32[]{:S(2)}, u32[]{:S(2)}) collective-permute-start(f32[2,8,3,4,1024]{4,3,2,1,0:T(4,128)} %get-tuple-element.335), channel_id=1, source_target_pairs={{1,0},{2,1},{3,2},{4,3},{5,4},{6,5},{7,6},{9,8},{10,9},{11,10},{12... | collective-permute-start | bytes 2359304 | tf_op jit(solution)/shard_map/ppermute | solution.py:36
  158.8 5.3 %collective-permute-done.6 = f32[2,8,3,4,1024]{4,3,2,1,0:T(4,128)} collective-permute-done((f32[2,8,3,4,1024]{4,3,2,1,0:T(4,128)}, f32[2,8,3,4,1024]{4,3,2,1,0:T(4,128)}, u32[]{:S(2)}, u32[]{:S(2)}) %collective-permute-start.6) | collective-permute-done | bytes 786464 | tf_op jit(solution)/shard_map/ppermute | solution.py:36
  164.1 8.9 %collective-permute-done.7 = f32[2,8,3,4,1024]{4,3,2,1,0:T(4,128)} collective-permute-done((f32[2,8,3,4,1024]{4,3,2,1,0:T(4,128)}, f32[2,8,3,4,1024]{4,3,2,1,0:T(4,128)}, u32[]{:S(2)}, u32[]{:S(2)}) %collective-permute-start.7) | collective-permute-done | bytes 786464 | tf_op jit(solution)/shard_map/ppermute | solution.py:36
  172.9 1.9 %fusion.24 = bf16[2,8,4,4,1024]{4,3,2,1,0:T(4,128)(2,1)S(1)} fusion(f32[2,8,10,4,1024]{4,3,2,1,0:T(4,128)S(1)} %fusion.22, f32[2,8,3,4,1024]{4,3,2,1,0:T(4,128)} %collective-permute-done.7, f32[2,8,3,4,1024]{4,3,2,1,0:T(4,128)} %collective-permute-done.6), kind=kLoop, calls=%fused_computation.54 | loop fusion | flops 786432 | bytes 3145728 | tf_op jit(solution)/shard_map/convert.5
  (220 shorter events, 61.6 us)
Async XLA Ops:
  2.0 7.6 %collective-permute-start = (bf16[2,3,4,4,1024]{4,3,2,1,0:T(4,128)(2,1)S(1)}, bf16[2,3,4,4,1024]{4,3,2,1,0:T(4,128)(2,1)S(1)}, u32[]{:S(2)}, u32[]{:S(2)}) collective-permute-start(bf16[2,3,4,4,1024]{4,3,2,1,0:T(4,128)(2,1)S(1)} %get-tuple-element.344), channel_id=1, source_target_pairs={{0,8},{8,16},{16,24},{1,9},{9,17},{17,25},{2,10},{10,18},{18,26},{... | collective-permute-start | bytes 589832 | tf_op jit(solution)/shard_map/ppermute | solution.py:24
  6.0 19.3 %copy-start.7 = (bf16[8,4,4,1024]{3,2,1,0:T(4,128)(2,1)S(1)}, bf16[8,4,4,1024]{3,2,1,0:T(4,128)(2,1)}, u32[]{:S(2)}) copy-start(bf16[8,4,4,1024]{3,2,1,0:T(4,128)(2,1)} %param.11) | copy-start | bytes 786436
  6.0 7.5 %collective-permute-start.1 = (bf16[2,3,4,4,1024]{4,3,2,1,0:T(4,128)(2,1)S(1)}, bf16[2,3,4,4,1024]{4,3,2,1,0:T(4,128)(2,1)S(1)}, u32[]{:S(2)}, u32[]{:S(2)}) collective-permute-start(bf16[2,3,4,4,1024]{4,3,2,1,0:T(4,128)(2,1)S(1)} %get-tuple-element.345), channel_id=1, source_target_pairs={{8,0},{16,8},{24,16},{9,1},{17,9},{25,17},{10,2},{18,10},{26,18},{... | collective-permute-start | bytes 589832 | tf_op jit(solution)/shard_map/ppermute | solution.py:26
  9.6 7.2 %copy-start.4 = (bf16[2,3,4,4,1024]{4,3,2,1,0:T(4,128)(2,1)}, bf16[2,3,4,4,1024]{4,3,2,1,0:T(4,128)(2,1)S(1)}, u32[]{:S(2)}) copy-start(bf16[2,3,4,4,1024]{4,3,2,1,0:T(4,128)(2,1)S(1)} %collective-permute-done) | copy-start | bytes 589828
  13.5 3.3 %copy-start.5 = (bf16[2,3,4,4,1024]{4,3,2,1,0:T(4,128)(2,1)}, bf16[2,3,4,4,1024]{4,3,2,1,0:T(4,128)(2,1)S(1)}, u32[]{:S(2)}) copy-start(bf16[2,3,4,4,1024]{4,3,2,1,0:T(4,128)(2,1)S(1)} %collective-permute-done.1) | copy-start | bytes 589828
  15.3 10.1 %copy-start.8 = (bf16[8,4,4,1024]{3,2,1,0:T(4,128)(2,1)S(1)}, bf16[8,4,4,1024]{3,2,1,0:T(4,128)(2,1)}, u32[]{:S(2)}) copy-start(bf16[8,4,4,1024]{3,2,1,0:T(4,128)(2,1)} %param.8) | copy-start | bytes 786436
  15.3 23.5 %copy-start.1 = (bf16[8,4,4,1024]{3,2,1,0:T(4,128)(2,1)S(1)}, bf16[8,4,4,1024]{3,2,1,0:T(4,128)(2,1)}, u32[]{:S(2)}) copy-start(bf16[8,4,4,1024]{3,2,1,0:T(4,128)(2,1)} %param.10) | copy-start | bytes 786436
  15.4 23.5 %copy-start.2 = (bf16[8,4,4,1024]{3,2,1,0:T(4,128)(2,1)S(1)}, bf16[8,4,4,1024]{3,2,1,0:T(4,128)(2,1)}, u32[]{:S(2)}) copy-start(bf16[8,4,4,1024]{3,2,1,0:T(4,128)(2,1)} %param.9) | copy-start | bytes 786436
  16.8 13.0 %collective-permute-start.2 = (bf16[2,14,3,4,1024]{4,3,2,1,0:T(4,128)(2,1)}, bf16[2,14,3,4,1024]{4,3,2,1,0:T(4,128)(2,1)S(1)}, u32[]{:S(2)}, u32[]{:S(2)}) collective-permute-start(bf16[2,14,3,4,1024]{4,3,2,1,0:T(4,128)(2,1)} %get-tuple-element.340), channel_id=1, source_target_pairs={{0,1},{1,2},{2,3},{3,4},{4,5},{5,6},{6,7},{8,9},{9,10},{10,11},{11... | collective-permute-start | bytes 2064392 | tf_op jit(solution)/shard_map/ppermute | solution.py:24
  21.6 17.2 %collective-permute-start.3 = (bf16[2,14,3,4,1024]{4,3,2,1,0:T(4,128)(2,1)S(1)}, bf16[2,14,3,4,1024]{4,3,2,1,0:T(4,128)(2,1)}, u32[]{:S(2)}, u32[]{:S(2)}) collective-permute-start(bf16[2,14,3,4,1024]{4,3,2,1,0:T(4,128)(2,1)S(1)} %get-tuple-element.341), channel_id=1, source_target_pairs={{1,0},{2,1},{3,2},{4,3},{5,4},{6,5},{7,6},{9,8},{10,9},{11,10},{12... | collective-permute-start | bytes 2064392 | tf_op jit(solution)/shard_map/ppermute | solution.py:26
  44.4 4.9 %copy-start = (bf16[1,14,10,4,1024]{4,3,2,1,0:T(4,128)(2,1)S(1)}, bf16[1,14,10,4,1024]{4,3,2,1,0:T(4,128)(2,1)}, u32[]{:S(2)}) copy-start(bf16[1,14,10,4,1024]{4,3,2,1,0:T(4,128)(2,1)} %get-tuple-element.339) | copy-start | bytes 3440644
  75.3 3.2 %copy-start.9 = (pred[560]{0:T(1024)(128)(4,1)}, pred[560]{0:T(1024)(128)(4,1)S(1)}, u32[]{:S(2)}) copy-start(pred[560]{0:T(1024)(128)(4,1)S(1)} %get-tuple-element.675) | copy-start | bytes 1684 | tf_op jit(solution)/shard_map/while
  75.3 3.2 %copy-start.13 = (f32[128,16]{0,1:T(8,128)}, f32[128,16]{0,1:T(8,128)S(1)}, u32[]{:S(2)}) copy-start(f32[128,16]{0,1:T(8,128)S(1)} %get-tuple-element.668) | copy-start | bytes 24580 | tf_op jit(solution)/shard_map/while
  75.3 3.2 %copy-start.15 = (s32[4]{0:T(128)}, s32[4]{0:T(128)S(1)}, u32[]{:S(2)}) copy-start(s32[4]{0:T(128)S(1)} %get-tuple-element.662) | copy-start | bytes 52 | tf_op jit(solution)/shard_map/while
  84.5 3.2 %copy-start.9 = (pred[560]{0:T(1024)(128)(4,1)}, pred[560]{0:T(1024)(128)(4,1)S(1)}, u32[]{:S(2)}) copy-start(pred[560]{0:T(1024)(128)(4,1)S(1)} %get-tuple-element.675) | copy-start | bytes 1684 | tf_op jit(solution)/shard_map/while
  84.5 3.2 %copy-start.13 = (f32[128,16]{0,1:T(8,128)}, f32[128,16]{0,1:T(8,128)S(1)}, u32[]{:S(2)}) copy-start(f32[128,16]{0,1:T(8,128)S(1)} %get-tuple-element.668) | copy-start | bytes 24580 | tf_op jit(solution)/shard_map/while
  84.5 3.2 %copy-start.15 = (s32[4]{0:T(128)}, s32[4]{0:T(128)S(1)}, u32[]{:S(2)}) copy-start(s32[4]{0:T(128)S(1)} %get-tuple-element.662) | copy-start | bytes 52 | tf_op jit(solution)/shard_map/while
  91.3 2.4 %copy-start.10 = (pred[560]{0:T(1024)(128)(4,1)S(1)}, pred[560]{0:T(1024)(128)(4,1)}, u32[]{:S(2)}) copy-start(pred[560]{0:T(1024)(128)(4,1)} %copy-done.9) | copy-start | bytes 1684 | tf_op jit(solution)/shard_map/while
  93.7 3.2 %copy-start.9 = (pred[560]{0:T(1024)(128)(4,1)}, pred[560]{0:T(1024)(128)(4,1)S(1)}, u32[]{:S(2)}) copy-start(pred[560]{0:T(1024)(128)(4,1)S(1)} %get-tuple-element.675) | copy-start | bytes 1684 | tf_op jit(solution)/shard_map/while
  93.8 3.2 %copy-start.13 = (f32[128,16]{0,1:T(8,128)}, f32[128,16]{0,1:T(8,128)S(1)}, u32[]{:S(2)}) copy-start(f32[128,16]{0,1:T(8,128)S(1)} %get-tuple-element.668) | copy-start | bytes 24580 | tf_op jit(solution)/shard_map/while
  93.8 3.2 %copy-start.15 = (s32[4]{0:T(128)}, s32[4]{0:T(128)S(1)}, u32[]{:S(2)}) copy-start(s32[4]{0:T(128)S(1)} %get-tuple-element.662) | copy-start | bytes 52 | tf_op jit(solution)/shard_map/while
  100.5 2.4 %copy-start.10 = (pred[560]{0:T(1024)(128)(4,1)S(1)}, pred[560]{0:T(1024)(128)(4,1)}, u32[]{:S(2)}) copy-start(pred[560]{0:T(1024)(128)(4,1)} %copy-done.9) | copy-start | bytes 1684 | tf_op jit(solution)/shard_map/while
  100.5 2.4 %copy-start.12 = (s32[128]{0:T(128)S(1)}, s32[128]{0:T(128)}, u32[]{:S(2)}) copy-start(s32[128]{0:T(128)} %copy-done.11) | copy-start | bytes 1540 | tf_op jit(solution)/shard_map/while
  103.0 3.2 %copy-start.9 = (pred[560]{0:T(1024)(128)(4,1)}, pred[560]{0:T(1024)(128)(4,1)S(1)}, u32[]{:S(2)}) copy-start(pred[560]{0:T(1024)(128)(4,1)S(1)} %get-tuple-element.675) | copy-start | bytes 1684 | tf_op jit(solution)/shard_map/while
  103.0 3.2 %copy-start.13 = (f32[128,16]{0,1:T(8,128)}, f32[128,16]{0,1:T(8,128)S(1)}, u32[]{:S(2)}) copy-start(f32[128,16]{0,1:T(8,128)S(1)} %get-tuple-element.668) | copy-start | bytes 24580 | tf_op jit(solution)/shard_map/while
  103.0 3.2 %copy-start.15 = (s32[4]{0:T(128)}, s32[4]{0:T(128)S(1)}, u32[]{:S(2)}) copy-start(s32[4]{0:T(128)S(1)} %get-tuple-element.662) | copy-start | bytes 52 | tf_op jit(solution)/shard_map/while
  109.8 2.4 %copy-start.10 = (pred[560]{0:T(1024)(128)(4,1)S(1)}, pred[560]{0:T(1024)(128)(4,1)}, u32[]{:S(2)}) copy-start(pred[560]{0:T(1024)(128)(4,1)} %copy-done.9) | copy-start | bytes 1684 | tf_op jit(solution)/shard_map/while
  131.7 9.2 %collective-permute-start.4 = (bf16[2,3,10,4,1024]{4,3,2,1,0:T(4,128)(2,1)S(1)}, bf16[2,3,10,4,1024]{4,3,2,1,0:T(4,128)(2,1)S(1)}, u32[]{:S(2)}, u32[]{:S(2)}) collective-permute-start(bf16[2,3,10,4,1024]{4,3,2,1,0:T(4,128)(2,1)S(1)} %get-tuple-element.336), channel_id=1, source_target_pairs={{0,8},{8,16},{16,24},{1,9},{9,17},{17,25},{2,10},{10,18},{18,26},{... | collective-permute-start | bytes 1474568 | tf_op jit(solution)/shard_map/ppermute | solution.py:36
  135.2 9.6 %collective-permute-start.5 = (bf16[2,3,10,4,1024]{4,3,2,1,0:T(4,128)(2,1)S(1)}, bf16[2,3,10,4,1024]{4,3,2,1,0:T(4,128)(2,1)S(1)}, u32[]{:S(2)}, u32[]{:S(2)}) collective-permute-start(bf16[2,3,10,4,1024]{4,3,2,1,0:T(4,128)(2,1)S(1)} %get-tuple-element.337), channel_id=1, source_target_pairs={{8,0},{16,8},{24,16},{9,1},{17,9},{25,17},{10,2},{18,10},{26,18},{... | collective-permute-start | bytes 1474568 | tf_op jit(solution)/shard_map/ppermute | solution.py:36
  145.7 12.1 %copy-start.3 = (bf16[4,128,256]{1,2,0:T(8,128)(2,1)S(1)}, bf16[4,128,256]{1,2,0:T(8,128)(2,1)}, u32[]{:S(2)}) copy-start(bf16[4,128,256]{1,2,0:T(8,128)(2,1)} %get-tuple-element.113) | copy-start | bytes 786436
  147.1 17.0 %collective-permute-start.6 = (f32[2,8,3,4,1024]{4,3,2,1,0:T(4,128)}, f32[2,8,3,4,1024]{4,3,2,1,0:T(4,128)}, u32[]{:S(2)}, u32[]{:S(2)}) collective-permute-start(f32[2,8,3,4,1024]{4,3,2,1,0:T(4,128)} %get-tuple-element.334), channel_id=1, source_target_pairs={{0,1},{1,2},{2,3},{3,4},{4,5},{5,6},{6,7},{8,9},{9,10},{10,11},{11... | collective-permute-start | bytes 2359304 | tf_op jit(solution)/shard_map/ppermute | solution.py:36
  154.8 18.1 %collective-permute-start.7 = (f32[2,8,3,4,1024]{4,3,2,1,0:T(4,128)}, f32[2,8,3,4,1024]{4,3,2,1,0:T(4,128)}, u32[]{:S(2)}, u32[]{:S(2)}) collective-permute-start(f32[2,8,3,4,1024]{4,3,2,1,0:T(4,128)} %get-tuple-element.335), channel_id=1, source_target_pairs={{1,0},{2,1},{3,2},{4,3},{5,4},{6,5},{7,6},{9,8},{10,9},{11,10},{12... | collective-permute-start | bytes 2359304 | tf_op jit(solution)/shard_map/ppermute | solution.py:36
  (17 other events, 37.4 us)
where the time goes:
time: 177 us; the launch traced here: 176 us
  local copies, waits for them, and re-layouts  59.1 us (33%)
  waiting for transfers between devices  40.7 us (23%)
  other arithmetic  27.1 us (15%)
  starting transfers between devices  26.7 us (15%)
  matrix products  12.4 us (7%)
  loops' own time  8.78 us (5%)
    ppermute x4, waiting for transfers between devices, from_behind(): return lax.ppermute(x, axis, pairs)  22.4 us
    ppermute x4, starting transfers between devices, from_behind(): return lax.ppermute(x, axis, pairs)  14.4 us
    ppermute x2, waiting for transfers between devices, padded(): lax.ppermute(head, axis, [((i + 1) % count, i) for i in range(ends)])  12.1 us
    and x8, other arithmetic, window_mask(): return within & inside  10.7 us
    ppermute x2, starting transfers between devices, padded(): lax.ppermute(tail, axis, [(i, (i + 1) % count) for i in range(ends)])  8.9 us
    transpose x4, local copies, waits for them, and re-layouts, regroup(): jnp.transpose(stacked, (1, 0, 2)).reshape(row_total, groups * group_width)  8.45 us
    another operation x3, local copies, waits for them, and re-layouts, on_device(): jnp.stack([part_k, part_v]).reshape(2, span_x, span_y, depth_z, features)  7.69 us
    unnamed x22, local copies, waits for them, and re-layouts  6.53 us
  transfers between devices with their start and end apart: 8, of which 8 were waited for; matrix products, arithmetic and copies ran while one was open for 2% of the time, Pallas kernels for 0%

commit v1 on v0

v1 whole, which is shorter than its diff:
```python
import functools

import jax
import jax.numpy as jnp
from jax import lax
from jax.experimental import pallas as pl
from jax.experimental.pallas import tpu as pltpu
from jax.sharding import PartitionSpec as P

HEADS = 16
RADIUS = 3
BLOCKED = -1e30
MESH = pl.DeviceIdType.MESH
NT = (((1,), (1,)), ((), ()))
TN = (((0,), (0,)), ((), ()))
NN = (((1,), (0,)), ((), ()))


def mm(a, b, dims):
    return lax.dot_general(a, b, dims, preferred_element_type=jnp.float32)


def kernel(
    ns, nt, q_ref, k_ref, v_ref, u_ref, o_ref, gq_ref, gk_ref, gv_ref,
    kv, bias, acc, zs, zr, ys, yr,
    ym_s, ym_r, z_s, z_r, zg_s, zg_r, yg_s, yg_r,
):
    G = kv.shape[0]
    si = lax.axis_index("space")
    ti = lax.axis_index("tp")
    has_lo, has_hi = si > 0, si < ns - 1
    has_l, has_r = ti > 0, ti < nt - 1
    lo, hi, left, right = (si - 1, ti), (si + 1, ti), (si, ti - 1), (si, ti + 1)

    barrier = pltpu.get_barrier_semaphore()
    for have, dev in ((has_lo, lo), (has_hi, hi), (has_l, left), (has_r, right)):
        @pl.when(have)
        def _(dev=dev):
            pl.semaphore_signal(barrier, inc=1, device_id=dev, device_id_type=MESH)

    def remote(src, dst, ss, rs, dev):
        return pltpu.make_async_remote_copy(
            src_ref=src, dst_ref=dst, send_sem=ss, recv_sem=rs, device_id=dev, device_id_type=MESH
        )

    def ymain(g):
        return (
            (remote(kv.at[g, :, 0:3, 0:2], kv.at[g, :, 7:10, 0:2], ym_s.at[g, 0], ym_r.at[g, 0], left), has_l, has_r),
            (remote(kv.at[g, :, 1:4, 0:2], kv.at[g, :, 4:7, 0:2], ym_s.at[g, 1], ym_r.at[g, 1], right), has_r, has_l),
        )

    def zmain(g):
        return (
            (remote(kv.at[g, :, :, 0], kv.at[g, :, :, 3], z_s.at[g, 0], z_r.at[g, 0], lo), has_lo, has_hi),
            (remote(kv.at[g, :, :, 1], kv.at[g, :, :, 2], z_s.at[g, 1], z_r.at[g, 1], hi), has_hi, has_lo),
        )

    def zgrad(g):
        return (
            (remote(zs.at[g, 0], zr.at[g, 0], zg_s.at[g, 0], zg_r.at[g, 0], lo), has_lo, has_hi),
            (remote(zs.at[g, 1], zr.at[g, 1], zg_s.at[g, 1], zg_r.at[g, 1], hi), has_hi, has_lo),
        )

    def ygrad(g):
        return (
            (remote(ys.at[g, 0], yr.at[g, 0], yg_s.at[g, 0], yg_r.at[g, 0], left), has_l, has_r),
            (remote(ys.at[g, 1], yr.at[g, 1], yg_s.at[g, 1], yg_r.at[g, 1], right), has_r, has_l),
        )

    def start(copies):
        for c, send, _r in copies:
            @pl.when(send)
            def _(c=c):
                c.start()

    def got(copies):
        for c, _s, recv in copies:
            @pl.when(recv)
            def _(c=c):
                c.wait_recv()

    def sent(copies):
        for c, send, _r in copies:
            @pl.when(send)
            def _(c=c):
                c.wait_send()

    def lanes(g):
        return pl.ds(pl.multiple_of(g * 128, 128), 128)

    r = lax.broadcasted_iota(jnp.int32, (128, 128), 0)
    c = lax.broadcasted_iota(jnp.int32, (128, 128), 1)
    want = ((r // 4) % 8) * 16 + (r // 32) * 4 + r % 4
    perm = jnp.where(c == want, 1.0, 0.0).astype(jnp.bfloat16)

    barrier_count = (
        has_lo.astype(jnp.int32) + has_hi.astype(jnp.int32) + has_l.astype(jnp.int32) + has_r.astype(jnp.int32)
    )

    def fill(g):
        for i, ref in enumerate((k_ref, v_ref)):
            own = mm(perm, ref[:, lanes(g)], NN).astype(jnp.bfloat16)
            kv[g, i, 0:4, 0:2] = own.reshape(4, 2, 16, 128)

    fill(0)
    pl.semaphore_wait(barrier, barrier_count)
    start(ymain(0))

    def prologue(g, carry):
        fill(g)
        start(ymain(g))
        return carry

    lax.fori_loop(1, G, prologue, 0)

    @pl.when(jnp.logical_not(has_l))
    def _():
        kv[:, :, 4:7, 0:2] = jnp.zeros((G, 2, 3, 2, 16, 128), jnp.bfloat16)

    @pl.when(jnp.logical_not(has_r))
    def _():
        kv[:, :, 7:10, 0:2] = jnp.zeros((G, 2, 3, 2, 16, 128), jnp.bfloat16)

    @pl.when(jnp.logical_not(has_lo))
    def _():
        kv[:, :, :, 2] = jnp.zeros((G, 2, 10, 16, 128), jnp.bfloat16)

    @pl.when(jnp.logical_not(has_hi))
    def _():
        kv[:, :, :, 3] = jnp.zeros((G, 2, 10, 16, 128), jnp.bfloat16)

    row = lax.broadcasted_iota(jnp.int32, (640, 128), 0)
    col = lax.broadcasted_iota(jnp.int32, (640, 128), 1)
    j, b, xi = row // 64, (row // 16) % 4, (row // 4) % 4
    ky = jnp.where(j < 4, j, jnp.where(j < 7, j - 7, j - 3))
    kx = jnp.where(b < 2, b * 4 + xi, jnp.where(b == 2, xi - 4, xi + 8))
    qx, qy = col // 16, (col // 4) % 4
    gx, gy = kx + si * 8, ky + ti * 4
    ok = (
        (jnp.abs(kx - qx) <= RADIUS) & (jnp.abs(ky - qy) <= RADIUS)
        & (gx >= 0) & (gx < ns * 8) & (gy >= 0) & (gy < nt * 4)
    )
    one = jnp.where(ok, 0.0, BLOCKED)
    bias[:, 0:128] = one
    bias[:, 128:256] = one

    lane = lax.broadcasted_iota(jnp.int32, (128, 128), 1)
    feat = lax.broadcasted_iota(jnp.int32, (128, 128), 0)

    def stacked(x):
        zero = jnp.zeros_like(x)
        return jnp.concatenate([jnp.where(lane < 64, x, zero), jnp.where(lane >= 64, x, zero)], axis=0).astype(jnp.bfloat16)

    def diagonal(x):
        return jnp.where(feat < 64, x[:, 0:128], x[:, 128:256])

    def forward(g):
        got(ymain(g))
        start(zmain(g))

    def compute(g):
        k = kv[g, 0].reshape(640, 128)
        v = kv[g, 1].reshape(640, 128)
        qf = q_ref[:, lanes(g)].astype(jnp.float32) * 0.125
        uf = u_ref[:, lanes(g)].astype(jnp.float32)
        qst, ust = stacked(qf), stacked(uf)
        s = mm(k, qst, NT) + bias[...]
        p = jnp.exp(s - jnp.max(s, axis=0, keepdims=True))
        w = p * (1.0 / jnp.sum(p, axis=0, keepdims=True))
        wb = w.astype(jnp.bfloat16)
        ot = diagonal(mm(v, wb, TN))
        o_ref[:, lanes(g)] = ot.T.astype(jnp.bfloat16)
        prod = uf.T * ot.astype(jnp.bfloat16).astype(jnp.float32)
        dots = jnp.concatenate(
            [jnp.sum(prod[0:64], axis=0, keepdims=True), jnp.sum(prod[64:128], axis=0, keepdims=True)], axis=1
        )
        ds = (w * (mm(v, ust, NT) - dots)).astype(jnp.bfloat16)
        gq_ref[:, lanes(g)] = (diagonal(mm(k, ds, TN)).T * 0.125).astype(jnp.bfloat16)
        for i, grad in enumerate((mm(ds, qst, NN), mm(wb, ust, NN))):
            grad = grad.reshape(10, 4, 16, 128)
            acc[g, i] = grad[:, 0:2]
            zs[g, 0, i] = grad[:, 2].astype(jnp.bfloat16)
            zs[g, 1, i] = grad[:, 3].astype(jnp.bfloat16)

    def stage_y(g):
        got(zgrad(g))

        @pl.when(has_hi)
        def _():
            acc[g, :, :, 1] += zr[g, 0].astype(jnp.float32)

        @pl.when(has_lo)
        def _():
            acc[g, :, :, 0] += zr[g, 1].astype(jnp.float32)

        ys[g, 0] = acc[g, :, 4:7].astype(jnp.bfloat16)
        ys[g, 1] = acc[g, :, 7:10].astype(jnp.bfloat16)
        start(ygrad(g))

    def stage_out(g):
        got(ygrad(g))

        @pl.when(has_r)
        def _():
            acc[g, :, 1:4] += yr[g, 0].astype(jnp.float32)

        @pl.when(has_l)
        def _():
            acc[g, :, 0:3] += yr[g, 1].astype(jnp.float32)

        for i, ref in enumerate((gk_ref, gv_ref)):
            own = acc[g, i, 0:4].reshape(128, 128).astype(jnp.bfloat16)
            ref[:, lanes(g)] = mm(perm, own, TN).astype(jnp.bfloat16)

    AHEAD = 2
    for g in range(AHEAD):
        forward(g)

    def step(g, carry):
        @pl.when(g + AHEAD < G)
        def _():
            forward(g + AHEAD)

        @pl.when(g < G)
        def _():
            got(zmain(g))
            compute(g)
            start(zgrad(g))

        @pl.when((g >= 1) & (g < G + 1))
        def _():
            stage_y(g - 1)

        @pl.when(g >= 3)
        def _():
            stage_out(g - 3)

        return carry

    lax.fori_loop(0, G + 3, step, 0)

    def drain(g, carry):
        for copies in (ymain(g), zmain(g), zgrad(g), ygrad(g)):
            sent(copies)
        return carry

    lax.fori_loop(0, G, drain, 0)


def on_device(queries, key_field, value_field, upstream):
    shape = queries.shape
    rows, feats = shape[0] * shape[1] * shape[2], shape[3]
    pairs = feats // 128
    flat = [x.reshape(rows, feats) for x in (queries, key_field, value_field, upstream)]
    vmem = pl.BlockSpec(memory_space=pltpu.VMEM)
    dma = lambda: pltpu.SemaphoreType.DMA((pairs, 2))
    outs = pl.pallas_call(
        functools.partial(kernel, lax.axis_size("space"), lax.axis_size("tp")),
        out_shape=[jax.ShapeDtypeStruct((rows, feats), jnp.bfloat16)] * 4,
        in_specs=[vmem] * 4,
        out_specs=[vmem] * 4,
        scratch_shapes=[
            pltpu.VMEM((pairs, 2, 10, 4, 16, 128), jnp.bfloat16),
            pltpu.VMEM((640, 256), jnp.float32),
            pltpu.VMEM((pairs, 2, 10, 2, 16, 128), jnp.float32),
            pltpu.VMEM((pairs, 2, 2, 10, 16, 128), jnp.bfloat16),
            pltpu.VMEM((pairs, 2, 2, 10, 16, 128), jnp.bfloat16),
            pltpu.VMEM((pairs, 2, 2, 3, 2, 16, 128), jnp.bfloat16),
            pltpu.VMEM((pairs, 2, 2, 3, 2, 16, 128), jnp.bfloat16),
        ] + [dma() for _ in range(8)],
        compiler_params=pltpu.CompilerParams(
            collective_id=0, has_side_effects=True, vmem_limit_bytes=48 * 1024 * 1024
        ),
        cost_estimate=pl.CostEstimate(flops=2 * 10**9, bytes_accessed=4 * 10**6, transcendentals=10**6),
        name="window_attention",
    )(*flat)
    return tuple(x.reshape(shape) for x in outs)


def solution(mesh):
    spec = P("space", "tp", None, None)
    return jax.shard_map(
        on_device, mesh=mesh, in_specs=(spec,) * 4, out_specs=(spec,) * 4, check_vma=False
    )
```

time: 177 us -> 50.6 us (0.29)
  local copies, waits for them, and re-layouts: 59.1 us -> 6.22 us
  Pallas kernels: 0 us -> 43.2 us
  waiting for transfers between devices: 40.7 us -> 0 us
  other arithmetic: 27.1 us -> 0 us
  starting transfers between devices: 26.7 us -> 0 us
  matrix products: 12.4 us -> 0 us
  loops' own time: 8.78 us -> 0 us
    pallas_call x0 -> x1, Pallas kernels: none -> 43.2 us  [on_device(): pl.pallas_call(functools.partial(kernel, lax.axis_size('space'), lax.axis...]
    ppermute x8 -> x0, waiting for transfers between devices: 40.7 us -> none  [the longest x4 22.4 us: from_behind(): return lax.ppermute(x, axis, pairs)]
    ppermute x8 -> x0, starting transfers between devices: 26.7 us -> none  [the longest x4 14.4 us: from_behind(): return lax.ppermute(x, axis, pairs)]
    another operation x9 -> x0, local copies, waits for them, and re-layouts: 14.5 us -> none  [the longest x3 7.69 us: on_device(): jnp.stack([part_k, part_v]).reshape(2, span_x, span_y, depth_z, features)]
    transpose x12 -> x0, local copies, waits for them, and re-layouts: 13.6 us -> none  [the longest x4 8.45 us: regroup(): jnp.transpose(stacked, (1, 0, 2)).reshape(row_total, groups * group_width)]
    dot_general x28 -> x0, matrix products: 12.4 us -> none  [the longest x8 6.11 us: one_group(): jnp.einsum('qhd,khd->hqk', query_part, key_part, preferred_element_type=j...]
    and x9 -> x0, other arithmetic: 10.7 us -> none  [the longest x8 10.7 us: window_mask(): return within & inside]
    another operation x2 -> x0, loops' own time: 8.78 us -> none  [the longest x1 5.92 us: attend_queries(): lax.map(one_group, jnp.arange(HEADS // heads_group, dtype=jnp.int32))]
  transfers between devices with their start and end apart: 8 -> 0, of which waited for: 8 -> 0; matrix products, arithmetic and copies ran while one was open for 2% -> 0% of each run, Pallas kernels for 0% -> 0%
where the time goes in v1:
time: 50.6 us; the launch traced here: 50.1 us
  Pallas kernels  43.2 us (85%)
  local copies, waits for them, and re-layouts  6.22 us (12%)
  between operations  0.68 us (1%)
    pallas_call x1, Pallas kernels, on_device(): pl.pallas_call(functools.partial(kernel, lax.axis_size('space'), lax.axis...  43.2 us
    reshape x4, local copies, waits for them, and re-layouts, on_device(): return tuple((x.reshape(shape) for x in outs))  3.22 us
    unnamed x6, local copies, waits for them, and re-layouts  1.76 us
    reshape x4, local copies, waits for them, and re-layouts, on_device(): x.reshape(rows, feats)  1.25 us

profile of v1, /device:TPU:1, one launch (start us, length us, event | category | flops | bytes accessed | tf_op | source)
XLA Modules:
  0.0 50.1 jit_solution(6422685471927359198)
XLA Ops:
  0.6 0.0 copy-start
  0.6 1.1 %reshape.32.q_ref = bf16[128,1024]{1,0:T(8,128)(2,1)S(1)} reshape(bf16[8,4,4,1024]{3,2,1,0:T(4,128)(2,1)} %param.4) | data formatting | bytes 524288 | tf_op jit(solution)/shard_map/reshape | solution.py:254
  1.7 0.0 copy-done
  1.7 0.0 copy-start.1
  1.7 0.1 reshape.33.k_ref
  1.8 0.9 %copy-done.1 = bf16[8,4,4,1024]{3,2,1,0:T(4,128)(2,1)S(1)} copy-done((bf16[8,4,4,1024]{3,2,1,0:T(4,128)(2,1)S(1)}, bf16[8,4,4,1024]{3,2,1,0:T(4,128)(2,1)}, u32[]{:S(2)}) %copy-start.1) | copy-done | bytes 262168
  2.7 0.0 copy-start.2
  2.7 0.1 reshape.34.v_ref
  2.7 0.9 %copy-done.2 = bf16[8,4,4,1024]{3,2,1,0:T(4,128)(2,1)S(1)} copy-done((bf16[8,4,4,1024]{3,2,1,0:T(4,128)(2,1)S(1)}, bf16[8,4,4,1024]{3,2,1,0:T(4,128)(2,1)}, u32[]{:S(2)}) %copy-start.2) | copy-done | bytes 262168
  3.6 0.1 reshape.35.u_ref
  3.7 43.2 %window_attention.1 = (bf16[128,1024]{1,0:T(8,128)(2,1)S(1)}, bf16[128,1024]{1,0:T(8,128)(2,1)S(1)}, bf16[128,1024]{1,0:T(8,128)(2,1)S(1)}, bf16[128,1024]{1,0:T(8,128)(2,1)S(1)}) custom-call(bf16[128,1024]{1,0:T(8,128)(2,1)S(1)} %reshape.32.q_ref, bf16[128,1024]{1,0:T(8,128)(2,1)S(1)} %reshape.33.k_ref, bf16[128,1024]{1,0:T(8,128)(2,1)S(1)} %reshape.34.v_ref, ...), custom_call_target="tpu_custom_call" | custom-call | flops 2000000000 | bytes 4000000 | tf_op jit(solution)/shard_map/window_attention/pallas_call | solution.py:257
  46.9 0.8 %reshape.36 = bf16[8,4,4,1024]{3,2,1,0:T(4,128)(2,1)} reshape(bf16[128,1024]{1,0:T(8,128)(2,1)S(1)} %get-tuple-element.8) | data formatting | bytes 524288 | tf_op jit(solution)/shard_map/reshape | solution.py:277
  47.7 0.8 %reshape.37 = bf16[8,4,4,1024]{3,2,1,0:T(4,128)(2,1)} reshape(bf16[128,1024]{1,0:T(8,128)(2,1)S(1)} %get-tuple-element.9) | data formatting | bytes 524288 | tf_op jit(solution)/shard_map/reshape | solution.py:277
  48.5 0.8 %reshape.38 = bf16[8,4,4,1024]{3,2,1,0:T(4,128)(2,1)} reshape(bf16[128,1024]{1,0:T(8,128)(2,1)S(1)} %get-tuple-element.10) | data formatting | bytes 524288 | tf_op jit(solution)/shard_map/reshape | solution.py:277
  49.3 0.8 %reshape.39 = bf16[8,4,4,1024]{3,2,1,0:T(4,128)(2,1)} reshape(bf16[128,1024]{1,0:T(8,128)(2,1)S(1)} %get-tuple-element.11) | data formatting | bytes 524288 | tf_op jit(solution)/shard_map/reshape | solution.py:277
Async XLA Ops:
  0.6 1.1 %copy-start = (bf16[8,4,4,1024]{3,2,1,0:T(4,128)(2,1)S(1)}, bf16[8,4,4,1024]{3,2,1,0:T(4,128)(2,1)}, u32[]{:S(2)}) copy-start(bf16[8,4,4,1024]{3,2,1,0:T(4,128)(2,1)} %param.5) | copy-start | bytes 786436
  1.7 1.0 %copy-start.1 = (bf16[8,4,4,1024]{3,2,1,0:T(4,128)(2,1)S(1)}, bf16[8,4,4,1024]{3,2,1,0:T(4,128)(2,1)}, u32[]{:S(2)}) copy-start(bf16[8,4,4,1024]{3,2,1,0:T(4,128)(2,1)} %param.6) | copy-start | bytes 786436
  2.7 0.9 %copy-start.2 = (bf16[8,4,4,1024]{3,2,1,0:T(4,128)(2,1)S(1)}, bf16[8,4,4,1024]{3,2,1,0:T(4,128)(2,1)}, u32[]{:S(2)}) copy-start(bf16[8,4,4,1024]{3,2,1,0:T(4,128)(2,1)} %param.7) | copy-start | bytes 786436

commit v2 on v1

--- a/solution.py
+++ b/solution.py
@@ -22,7 +22,7 @@
 
 def kernel(
     ns, nt, q_ref, k_ref, v_ref, u_ref, o_ref, gq_ref, gk_ref, gv_ref,
-    kv, bias, acc, zs, zr, ys, yr,
+    kv, pack, rim, kmask, qmask, acc, zs, zr, ys, yr,
     ym_s, ym_r, z_s, z_r, zg_s, zg_r, yg_s, yg_r,
 ):
     G = kv.shape[0]
@@ -45,14 +45,14 @@
 
     def ymain(g):
         return (
-            (remote(kv.at[g, :, 0:3, 0:2], kv.at[g, :, 7:10, 0:2], ym_s.at[g, 0], ym_r.at[g, 0], left), has_l, has_r),
-            (remote(kv.at[g, :, 1:4, 0:2], kv.at[g, :, 4:7, 0:2], ym_s.at[g, 1], ym_r.at[g, 1], right), has_r, has_l),
+            (remote(kv.at[g, :, 0:3], kv.at[g, :, 7:10], ym_s.at[g, 0], ym_r.at[g, 0], left), has_l, has_r),
+            (remote(kv.at[g, :, 1:4], kv.at[g, :, 4:7], ym_s.at[g, 1], ym_r.at[g, 1], right), has_r, has_l),
         )
 
     def zmain(g):
         return (
-            (remote(kv.at[g, :, :, 0], kv.at[g, :, :, 3], z_s.at[g, 0], z_r.at[g, 0], lo), has_lo, has_hi),
-            (remote(kv.at[g, :, :, 1], kv.at[g, :, :, 2], z_s.at[g, 1], z_r.at[g, 1], hi), has_hi, has_lo),
+            (remote(pack.at[g, 0], rim.at[g, 1], z_s.at[g, 0], z_r.at[g, 0], lo), has_lo, has_hi),
+            (remote(pack.at[g, 1], rim.at[g, 0], z_s.at[g, 1], z_r.at[g, 1], hi), has_hi, has_lo),
         )
 
     def zgrad(g):
@@ -97,10 +97,26 @@
         has_lo.astype(jnp.int32) + has_hi.astype(jnp.int32) + has_l.astype(jnp.int32) + has_r.astype(jnp.int32)
     )
 
+    def choose(packed, cell, first):
+        hit = (cell == (packed // 12) * 16 + packed % 12 + first) & (packed < 120)
+        return jnp.where(hit, 1.0, 0.0).astype(jnp.bfloat16)
+
+    def iota(shape, dim):
+        return lax.broadcasted_iota(jnp.int32, shape, dim)
+
+    packs = [choose(iota((128, 160), 0), iota((128, 160), 1), 4 * i) for i in range(2)]
+    unpacks = [choose(iota((160, 128), 1), iota((160, 128), 0), 4 * i) for i in range(2)]
+
+    def cells(ref, g):
+        return ref[:, :, :, lanes(g)].astype(jnp.float32).reshape(128, 128)
+
+    def put(ref, g, x):
+        ref[:, :, :, lanes(g)] = x.reshape(8, 4, 4, 128).astype(jnp.bfloat16)
+
     def fill(g):
         for i, ref in enumerate((k_ref, v_ref)):
-            own = mm(perm, ref[:, lanes(g)], NN).astype(jnp.bfloat16)
-            kv[g, i, 0:4, 0:2] = own.reshape(4, 2, 16, 128)
+            own = mm(perm, cells(ref, g).astype(jnp.bfloat16), NN).astype(jnp.bfloat16)
+            kv[g, i, 0:4] = own.reshape(4, 2, 16, 128)
 
     fill(0)
     pl.semaphore_wait(barrier, barrier_count)
@@ -115,34 +131,39 @@
 
     @pl.when(jnp.logical_not(has_l))
     def _():
-        kv[:, :, 4:7, 0:2] = jnp.zeros((G, 2, 3, 2, 16, 128), jnp.bfloat16)
+        kv[:, :, 4:7] = jnp.zeros((G, 2, 3, 2, 16, 128), jnp.bfloat16)
 
     @pl.when(jnp.logical_not(has_r))
     def _():
-        kv[:, :, 7:10, 0:2] = jnp.zeros((G, 2, 3, 2, 16, 128), jnp.bfloat16)
+        kv[:, :, 7:10] = jnp.zeros((G, 2, 3, 2, 16, 128), jnp.bfloat16)
 
     @pl.when(jnp.logical_not(has_lo))
     def _():
-        kv[:, :, :, 2] = jnp.zeros((G, 2, 10, 16, 128), jnp.bfloat16)
+        rim[:, 0] = jnp.zeros((G, 2, 128, 128), jnp.bfloat16)
 
     @pl.when(jnp.logical_not(has_hi))
     def _():
-        kv[:, :, :, 3] = jnp.zeros((G, 2, 10, 16, 128), jnp.bfloat16)
-
-    row = lax.broadcasted_iota(jnp.int32, (640, 128), 0)
-    col = lax.broadcasted_iota(jnp.int32, (640, 128), 1)
-    j, b, xi = row // 64, (row // 16) % 4, (row // 4) % 4
+        rim[:, 1] = jnp.zeros((G, 2, 128, 128), jnp.bfloat16)
+
+    row, f = iota((576, 128), 0), iota((576, 128), 1)
+    low, high = row < 128, row >= 448
+    t = jnp.where(low, row, jnp.where(high, row - 448, row - 128))
+    edge = low | high
+    j = jnp.where(edge, t // 12, t // 32)
+    spare = edge & (t >= 120)
     ky = jnp.where(j < 4, j, jnp.where(j < 7, j - 7, j - 3))
-    kx = jnp.where(b < 2, b * 4 + xi, jnp.where(b == 2, xi - 4, xi + 8))
+    kx = jnp.where(low, (t % 12) // 4 - 3, jnp.where(high, (t % 12) // 4 + 8, (t % 32) // 4))
+    on = (spare & (f == 32)) | (jnp.logical_not(spare) & ((f == kx + 3) | (f == ky + 19)))
+    kmask[...] = jnp.where(on, 1.0, 0.0).astype(jnp.bfloat16)
+
+    col, f = iota((256, 128), 0) % 128, iota((256, 128), 1)
     qx, qy = col // 16, (col // 4) % 4
+    kx, ky = f - 3, f - 19
     gx, gy = kx + si * 8, ky + ti * 4
-    ok = (
-        (jnp.abs(kx - qx) <= RADIUS) & (jnp.abs(ky - qy) <= RADIUS)
-        & (gx >= 0) & (gx < ns * 8) & (gy >= 0) & (gy < nt * 4)
-    )
-    one = jnp.where(ok, 0.0, BLOCKED)
-    bias[:, 0:128] = one
-    bias[:, 128:256] = one
+    far_x = (jnp.abs(kx - qx) > RADIUS) | (gx < 0) | (gx >= ns * 8)
+    far_y = (jnp.abs(ky - qy) > RADIUS) | (gy < 0) | (gy >= nt * 4)
+    off = ((f < 14) & far_x) | ((f >= 16) & (f < 26) & far_y) | (f == 32)
+    qmask[...] = jnp.where(off, BLOCKED, 0.0).astype(jnp.bfloat16)
 
     lane = lax.broadcasted_iota(jnp.int32, (128, 128), 1)
     feat = lax.broadcasted_iota(jnp.int32, (128, 128), 0)
@@ -156,42 +177,55 @@
 
     def forward(g):
         got(ymain(g))
+        for i in range(2):
+            both = jnp.concatenate([kv[g, 0, :, i].reshape(160, 128), kv[g, 1, :, i].reshape(160, 128)], axis=1)
+            out = mm(packs[i], both, NN).astype(jnp.bfloat16)
+            pack[g, i, 0] = out[:, 0:128]
+            pack[g, i, 1] = out[:, 128:256]
         start(zmain(g))
 
     def compute(g):
-        k = kv[g, 0].reshape(640, 128)
-        v = kv[g, 1].reshape(640, 128)
-        qf = q_ref[:, lanes(g)].astype(jnp.float32) * 0.125
-        uf = u_ref[:, lanes(g)].astype(jnp.float32)
-        qst, ust = stacked(qf), stacked(uf)
-        s = mm(k, qst, NT) + bias[...]
+        def all_rows(i):
+            return jnp.concatenate([rim[g, 0, i], kv[g, i].reshape(320, 128), rim[g, 1, i]], axis=0)
+
+        k, v = all_rows(0), all_rows(1)
+        qf, uf = cells(q_ref, g) * 0.125, cells(u_ref, g)
+        s = mm(
+            jnp.concatenate([k, kmask[...]], axis=1), jnp.concatenate([stacked(qf), qmask[...]], axis=1), NT
+        )
         p = jnp.exp(s - jnp.max(s, axis=0, keepdims=True))
-        w = p * (1.0 / jnp.sum(p, axis=0, keepdims=True))
-        wb = w.astype(jnp.bfloat16)
-        ot = diagonal(mm(v, wb, TN))
-        o_ref[:, lanes(g)] = ot.T.astype(jnp.bfloat16)
+        inv = 1.0 / jnp.sum(p, axis=0, keepdims=True)
+        inv = jnp.where(feat < 64, inv[:, 0:128], inv[:, 128:256])
+        pb = p.astype(jnp.bfloat16)
+        ot = diagonal(mm(v, pb, TN)) * inv
+        put(o_ref, g, ot.T)
         prod = uf.T * ot.astype(jnp.bfloat16).astype(jnp.float32)
         dots = jnp.concatenate(
             [jnp.sum(prod[0:64], axis=0, keepdims=True), jnp.sum(prod[64:128], axis=0, keepdims=True)], axis=1
         )
-        ds = (w * (mm(v, ust, NT) - dots)).astype(jnp.bfloat16)
-        gq_ref[:, lanes(g)] = (diagonal(mm(k, ds, TN)).T * 0.125).astype(jnp.bfloat16)
-        for i, grad in enumerate((mm(ds, qst, NN), mm(wb, ust, NN))):
-            grad = grad.reshape(10, 4, 16, 128)
-            acc[g, i] = grad[:, 0:2]
-            zs[g, 0, i] = grad[:, 2].astype(jnp.bfloat16)
-            zs[g, 1, i] = grad[:, 3].astype(jnp.bfloat16)
+        ds = (p * (mm(v, stacked(uf), NT) - dots)).astype(jnp.bfloat16)
+        put(gq_ref, g, (diagonal(mm(k, ds, TN)) * (inv * 0.125)).T)
+        inv = inv.T
+        for i, grad in enumerate((mm(ds, stacked(qf * inv), NN), mm(pb, stacked(uf * inv), NN))):
+            acc[g, i] = grad[128:448].reshape(10, 2, 16, 128)
+            zs[g, 0, i] = grad[0:128].astype(jnp.bfloat16)
+            zs[g, 1, i] = grad[448:576].astype(jnp.bfloat16)
+
+    def unpack(g, side, block):
+        both = mm(unpacks[block], jnp.concatenate([zr[g, side, 0], zr[g, side, 1]], axis=1), NN)
+        acc[g, 0, :, block] += both[:, 0:128].reshape(10, 16, 128)
+        acc[g, 1, :, block] += both[:, 128:256].reshape(10, 16, 128)
 
     def stage_y(g):
         got(zgrad(g))
 
         @pl.when(has_hi)
         def _():
-            acc[g, :, :, 1] += zr[g, 0].astype(jnp.float32)
+            unpack(g, 0, 1)
 
         @pl.when(has_lo)
         def _():
-            acc[g, :, :, 0] += zr[g, 1].astype(jnp.float32)
+            unpack(g, 1, 0)
 
         ys[g, 0] = acc[g, :, 4:7].astype(jnp.bfloat16)
         ys[g, 1] = acc[g, :, 7:10].astype(jnp.bfloat16)
@@ -210,7 +244,7 @@
 
         for i, ref in enumerate((gk_ref, gv_ref)):
             own = acc[g, i, 0:4].reshape(128, 128).astype(jnp.bfloat16)
-            ref[:, lanes(g)] = mm(perm, own, TN).astype(jnp.bfloat16)
+            put(ref, g, mm(perm, own, TN))
 
     AHEAD = 2
     for g in range(AHEAD):
@@ -249,22 +283,23 @@
 
 def on_device(queries, key_field, value_field, upstream):
     shape = queries.shape
-    rows, feats = shape[0] * shape[1] * shape[2], shape[3]
-    pairs = feats // 128
-    flat = [x.reshape(rows, feats) for x in (queries, key_field, value_field, upstream)]
+    pairs = shape[3] // 128
     vmem = pl.BlockSpec(memory_space=pltpu.VMEM)
     dma = lambda: pltpu.SemaphoreType.DMA((pairs, 2))
     outs = pl.pallas_call(
         functools.partial(kernel, lax.axis_size("space"), lax.axis_size("tp")),
-        out_shape=[jax.ShapeDtypeStruct((rows, feats), jnp.bfloat16)] * 4,
+        out_shape=[jax.ShapeDtypeStruct(shape, jnp.bfloat16)] * 4,
         in_specs=[vmem] * 4,
         out_specs=[vmem] * 4,
         scratch_shapes=[
-            pltpu.VMEM((pairs, 2, 10, 4, 16, 128), jnp.bfloat16),
-            pltpu.VMEM((640, 256), jnp.float32),
+            pltpu.VMEM((pairs, 2, 10, 2, 16, 128), jnp.bfloat16),
+            pltpu.VMEM((pairs, 2, 2, 128, 128), jnp.bfloat16),
+            pltpu.VMEM((pairs, 2, 2, 128, 128), jnp.bfloat16),
+            pltpu.VMEM((576, 128), jnp.bfloat16),
+            pltpu.VMEM((256, 128), jnp.bfloat16),
             pltpu.VMEM((pairs, 2, 10, 2, 16, 128), jnp.float32),
-            pltpu.VMEM((pairs, 2, 2, 10, 16, 128), jnp.bfloat16),
-            pltpu.VMEM((pairs, 2, 2, 10, 16, 128), jnp.bfloat16),
+            pltpu.VMEM((pairs, 2, 2, 128, 128), jnp.bfloat16),
+            pltpu.VMEM((pairs, 2, 2, 128, 128), jnp.bfloat16),
             pltpu.VMEM((pairs, 2, 2, 3, 2, 16, 128), jnp.bfloat16),
             pltpu.VMEM((pairs, 2, 2, 3, 2, 16, 128), jnp.bfloat16),
         ] + [dma() for _ in range(8)],
@@ -273,8 +308,8 @@
         ),
         cost_estimate=pl.CostEstimate(flops=2 * 10**9, bytes_accessed=4 * 10**6, transcendentals=10**6),
         name="window_attention",
-    )(*flat)
-    return tuple(x.reshape(shape) for x in outs)
+    )(queries, key_field, value_field, upstream)
+    return tuple(outs)
 
 
 def solution(mesh):

time: 50.6 us -> 47.2 us (0.933)
  the two profiles are of different devices: /device:TPU:1 before, /device:TPU:3 now
where the time goes in v2:
time: 47.2 us; the launch traced here: 47 us
  Pallas kernels  39.7 us (84%)
  local copies, waits for them, and re-layouts  6.6 us (14%)
  between operations  0.65 us (1%)
    pallas_call x1, Pallas kernels, on_device(): pl.pallas_call(functools.partial(kernel, lax.axis_size('space'), lax.axis...  39.7 us
    unnamed x12, local copies, waits for them, and re-layouts  6.6 us

profile of v2, /device:TPU:3, one launch (start us, length us, event | category | flops | bytes accessed | tf_op | source)
XLA Modules:
  0.0 47.0 jit_solution(6507001441724232926)
XLA Ops:
  0.6 0.0 copy-start
  0.6 0.9 %copy-done = bf16[8,4,4,1024]{3,2,1,0:T(4,128)(2,1)S(1)} copy-done((bf16[8,4,4,1024]{3,2,1,0:T(4,128)(2,1)S(1)}, bf16[8,4,4,1024]{3,2,1,0:T(4,128)(2,1)}, u32[]{:S(2)}) %copy-start) | copy-done | bytes 262168
  1.6 0.0 copy-start.1
  1.6 0.9 %copy-done.1 = bf16[8,4,4,1024]{3,2,1,0:T(4,128)(2,1)S(1)} copy-done((bf16[8,4,4,1024]{3,2,1,0:T(4,128)(2,1)S(1)}, bf16[8,4,4,1024]{3,2,1,0:T(4,128)(2,1)}, u32[]{:S(2)}) %copy-start.1) | copy-done | bytes 262168
  2.5 0.0 copy-start.2
  2.5 0.9 %copy-done.2 = bf16[8,4,4,1024]{3,2,1,0:T(4,128)(2,1)S(1)} copy-done((bf16[8,4,4,1024]{3,2,1,0:T(4,128)(2,1)S(1)}, bf16[8,4,4,1024]{3,2,1,0:T(4,128)(2,1)}, u32[]{:S(2)}) %copy-start.2) | copy-done | bytes 262168
  3.5 0.0 copy-start.3
  3.5 0.9 %copy-done.3 = bf16[8,4,4,1024]{3,2,1,0:T(4,128)(2,1)S(1)} copy-done((bf16[8,4,4,1024]{3,2,1,0:T(4,128)(2,1)S(1)}, bf16[8,4,4,1024]{3,2,1,0:T(4,128)(2,1)}, u32[]{:S(2)}) %copy-start.3) | copy-done | bytes 262168
  4.4 39.7 %window_attention.1 = (bf16[8,4,4,1024]{3,2,1,0:T(4,128)(2,1)S(1)}, bf16[8,4,4,1024]{3,2,1,0:T(4,128)(2,1)S(1)}, bf16[8,4,4,1024]{3,2,1,0:T(4,128)(2,1)S(1)}, bf16[8,4,4,1024]{3,2,1,0:T(4,128)(2,1)S(1)}) custom-call(bf16[8,4,4,1024]{3,2,1,0:T(4,128)(2,1)S(1)} %copy-done, bf16[8,4,4,1024]{3,2,1,0:T(4,128)(2,1)S(1)} %copy-done.1, ...), custom_call_target="tpu_custom_call" | custom-call | flops 2000000000 | bytes 4000000 | tf_op jit(solution)/shard_map/window_attention/pallas_call | solution.py:289
  44.1 0.7 %copy.12 = bf16[8,4,4,1024]{3,2,1,0:T(4,128)(2,1)} copy(bf16[8,4,4,1024]{3,2,1,0:T(4,128)(2,1)S(1)} %get-tuple-element.8) | data formatting | bytes 524288
  44.9 0.7 %copy.13 = bf16[8,4,4,1024]{3,2,1,0:T(4,128)(2,1)} copy(bf16[8,4,4,1024]{3,2,1,0:T(4,128)(2,1)S(1)} %get-tuple-element.9) | data formatting | bytes 524288
  45.6 0.7 %copy.14 = bf16[8,4,4,1024]{3,2,1,0:T(4,128)(2,1)} copy(bf16[8,4,4,1024]{3,2,1,0:T(4,128)(2,1)S(1)} %get-tuple-element.10) | data formatting | bytes 524288
  46.3 0.7 %copy.15 = bf16[8,4,4,1024]{3,2,1,0:T(4,128)(2,1)} copy(bf16[8,4,4,1024]{3,2,1,0:T(4,128)(2,1)S(1)} %get-tuple-element.11) | data formatting | bytes 524288
Async XLA Ops:
  0.6 1.0 %copy-start = (bf16[8,4,4,1024]{3,2,1,0:T(4,128)(2,1)S(1)}, bf16[8,4,4,1024]{3,2,1,0:T(4,128)(2,1)}, u32[]{:S(2)}) copy-start(bf16[8,4,4,1024]{3,2,1,0:T(4,128)(2,1)} %q_ref.1) | copy-start | bytes 786436
  1.6 0.9 %copy-start.1 = (bf16[8,4,4,1024]{3,2,1,0:T(4,128)(2,1)S(1)}, bf16[8,4,4,1024]{3,2,1,0:T(4,128)(2,1)}, u32[]{:S(2)}) copy-start(bf16[8,4,4,1024]{3,2,1,0:T(4,128)(2,1)} %k_ref.1) | copy-start | bytes 786436
  2.5 0.9 %copy-start.2 = (bf16[8,4,4,1024]{3,2,1,0:T(4,128)(2,1)S(1)}, bf16[8,4,4,1024]{3,2,1,0:T(4,128)(2,1)}, u32[]{:S(2)}) copy-start(bf16[8,4,4,1024]{3,2,1,0:T(4,128)(2,1)} %v_ref.1) | copy-start | bytes 786436
  3.5 0.9 %copy-start.3 = (bf16[8,4,4,1024]{3,2,1,0:T(4,128)(2,1)S(1)}, bf16[8,4,4,1024]{3,2,1,0:T(4,128)(2,1)}, u32[]{:S(2)}) copy-start(bf16[8,4,4,1024]{3,2,1,0:T(4,128)(2,1)} %u_ref.1) | copy-start | bytes 786436

commit v3 on v2

v3 whole, which is shorter than its diff:
```python
import functools

import jax
import jax.numpy as jnp
from jax import lax
from jax.experimental import pallas as pl
from jax.experimental.pallas import tpu as pltpu
from jax.sharding import PartitionSpec as P

HEADS = 16
RADIUS = 3
BLOCKED = -1e30
MESH = pl.DeviceIdType.MESH
NT = (((1,), (1,)), ((), ()))
TN = (((0,), (0,)), ((), ()))
NN = (((1,), (0,)), ((), ()))


def mm(a, b, dims):
    return lax.dot_general(a, b, dims, preferred_element_type=jnp.float32)


def kernel(
    ns, nt, q_hbm, k_hbm, v_hbm, u_hbm, o_ref, gq_ref, gk_ref, gv_ref,
    q_ref, k_ref, v_ref, u_ref, kv, pack, rim, kmask, qmask, acc, zs, zr, ys, yr,
    ym_s, ym_r, z_s, z_r, zg_s, zg_r, yg_s, yg_r, zo_s, zo_r, zgo_s, zgo_r, in_s,
):
    G = kv.shape[0]
    si = lax.axis_index("space")
    ti = lax.axis_index("tp")
    has_lo, has_hi = si > 0, si < ns - 1
    has_l, has_r = ti > 0, ti < nt - 1
    lo, hi, left, right = (si - 1, ti), (si + 1, ti), (si, ti - 1), (si, ti + 1)

    loads = [
        pltpu.make_async_copy(src, dst, in_s.at[i])
        for i, (src, dst) in enumerate(((k_hbm, k_ref), (v_hbm, v_ref), (q_hbm, q_ref), (u_hbm, u_ref)))
    ]
    for load in loads:
        load.start()

    barrier = pltpu.get_barrier_semaphore()
    for have, dev in ((has_lo, lo), (has_hi, hi), (has_l, left), (has_r, right)):
        @pl.when(have)
        def _(dev=dev):
            pl.semaphore_signal(barrier, inc=1, device_id=dev, device_id_type=MESH)

    def remote(src, dst, ss, rs, dev):
        return pltpu.make_async_remote_copy(
            src_ref=src, dst_ref=dst, send_sem=ss, recv_sem=rs, device_id=dev, device_id_type=MESH
        )

    def ymain(g):
        return (
            (remote(kv.at[g, :, 0:3], kv.at[g, :, 7:10], ym_s.at[g, 0], ym_r.at[g, 0], left), has_l, has_r),
            (remote(kv.at[g, :, 1:4], kv.at[g, :, 4:7], ym_s.at[g, 1], ym_r.at[g, 1], right), has_r, has_l),
        )

    def along_z(src, dst, ss, rs, g, rows, flip):
        return tuple(
            (
                remote(src.at[g, i, :, rows], dst.at[g, 1 - i if flip else i, :, rows], ss.at[g, i], rs.at[g, i], dev),
                send,
                recv,
            )
            for i, dev, send, recv in ((0, lo, has_lo, has_hi), (1, hi, has_hi, has_lo))
        )

    own_rows, corner_rows = pl.ds(0, 48), pl.ds(48, 80)

    def zown(g):
        return along_z(pack, rim, zo_s, zo_r, g, own_rows, True)

    def zcorner(g):
        return along_z(pack, rim, z_s, z_r, g, corner_rows, True)

    def zgrad_own(g):
        return along_z(zs, zr, zgo_s, zgo_r, g, own_rows, False)

    def zgrad_corner(g):
        return along_z(zs, zr, zg_s, zg_r, g, corner_rows, False)

    def ygrad(g):
        return (
            (remote(ys.at[g, 0], yr.at[g, 0], yg_s.at[g, 0], yg_r.at[g, 0], left), has_l, has_r),
            (remote(ys.at[g, 1], yr.at[g, 1], yg_s.at[g, 1], yg_r.at[g, 1], right), has_r, has_l),
        )

    def start(copies):
        for c, send, _r in copies:
            @pl.when(send)
            def _(c=c):
                c.start()

    def got(copies):
        for c, _s, recv in copies:
            @pl.when(recv)
            def _(c=c):
                c.wait_recv()

    def sent(copies):
        for c, send, _r in copies:
            @pl.when(send)
            def _(c=c):
                c.wait_send()

    def lanes(g):
        return pl.ds(pl.multiple_of(g * 128, 128), 128)

    def iota(shape, dim):
        return lax.broadcasted_iota(jnp.int32, shape, dim)

    r = iota((224, 128), 0)
    t = jnp.where(r >= 176, r - 176, r - 128)
    x = jnp.where(r < 128, (r // 4) % 8, (t % 12) // 4 + jnp.where(r >= 176, 5, 0))
    y = jnp.where(r < 128, r // 32, t // 12)
    spread = jnp.where(iota((224, 128), 1) == x * 16 + y * 4 + r % 4, 1.0, 0.0).astype(jnp.bfloat16)
    r, c = iota((128, 128), 0), iota((128, 128), 1)
    perm = jnp.where(c == ((r // 4) % 8) * 16 + (r // 32) * 4 + r % 4, 1.0, 0.0).astype(jnp.bfloat16)

    barrier_count = (
        has_lo.astype(jnp.int32) + has_hi.astype(jnp.int32) + has_l.astype(jnp.int32) + has_r.astype(jnp.int32)
    )

    def choose(packed, cell, first, used):
        hit = (cell == (packed // 12) * 16 + packed % 12 + first) & (packed < used)
        return jnp.where(hit, 1.0, 0.0).astype(jnp.bfloat16)

    packs = [choose(iota((80, 96), 0), iota((80, 96), 1), 4 * i, 72) for i in range(2)]
    unpacks = [choose(iota((96, 80), 1), iota((96, 80), 0), 4 * i, 72) for i in range(2)]
    unpacks_own = [choose(iota((64, 48), 1), iota((64, 48), 0), 4 * i, 48) for i in range(2)]

    def cells(ref, g):
        return ref[:, :, :, lanes(g)].astype(jnp.float32).reshape(128, 128)

    def put(ref, g, x):
        ref[:, :, :, lanes(g)] = x.reshape(8, 4, 4, 128).astype(jnp.bfloat16)

    def fill(g):
        both = jnp.concatenate([cells(k_ref, g), cells(v_ref, g)], axis=1).astype(jnp.bfloat16)
        out = mm(spread, both, NN).astype(jnp.bfloat16)
        for i in range(2):
            part = out[:, 128 * i : 128 * i + 128]
            kv[g, i, 0:4] = part[0:128].reshape(4, 2, 16, 128)
            pack[g, 0, i, 0:48] = part[128:176]
            pack[g, 1, i, 0:48] = part[176:224]

    loads[0].wait()
    loads[1].wait()
    fill(0)
    pl.semaphore_wait(barrier, barrier_count)
    start(ymain(0))
    start(zown(0))

    def prologue(g, carry):
        fill(g)
        start(ymain(g))
        start(zown(g))
        return carry

    lax.fori_loop(1, G, prologue, 0)

    @pl.when(jnp.logical_not(has_l))
    def _():
        kv[:, :, 4:7] = jnp.zeros((G, 2, 3, 2, 16, 128), jnp.bfloat16)

    @pl.when(jnp.logical_not(has_r))
    def _():
        kv[:, :, 7:10] = jnp.zeros((G, 2, 3, 2, 16, 128), jnp.bfloat16)

    @pl.when(jnp.logical_not(has_lo))
    def _():
        rim[:, 0] = jnp.zeros((G, 2, 128, 128), jnp.bfloat16)

    @pl.when(jnp.logical_not(has_hi))
    def _():
        rim[:, 1] = jnp.zeros((G, 2, 128, 128), jnp.bfloat16)

    row, f = iota((576, 128), 0), iota((576, 128), 1)
    low, high = row < 128, row >= 448
    t = jnp.where(low, row, jnp.where(high, row - 448, row - 128))
    edge = low | high
    j = jnp.where(edge, t // 12, t // 32)
    spare = edge & (t >= 120)
    ky = jnp.where(j < 4, j, jnp.where(j < 7, j - 7, j - 3))
    kx = jnp.where(low, (t % 12) // 4 - 3, jnp.where(high, (t % 12) // 4 + 8, (t % 32) // 4))
    on = (spare & (f == 32)) | (jnp.logical_not(spare) & ((f == kx + 3) | (f == ky + 19)))
    kmask[...] = jnp.where(on, 1.0, 0.0).astype(jnp.bfloat16)

    col, f = iota((256, 128), 0) % 128, iota((256, 128), 1)
    qx, qy = col // 16, (col // 4) % 4
    kx, ky = f - 3, f - 19
    gx, gy = kx + si * 8, ky + ti * 4
    far_x = (jnp.abs(kx - qx) > RADIUS) | (gx < 0) | (gx >= ns * 8)
    far_y = (jnp.abs(ky - qy) > RADIUS) | (gy < 0) | (gy >= nt * 4)
    off = ((f < 14) & far_x) | ((f >= 16) & (f < 26) & far_y) | (f == 32)
    qmask[...] = jnp.where(off, BLOCKED, 0.0).astype(jnp.bfloat16)

    lane = lax.broadcasted_iota(jnp.int32, (128, 128), 1)
    feat = lax.broadcasted_iota(jnp.int32, (128, 128), 0)

    def stacked(x):
        zero = jnp.zeros_like(x)
        return jnp.concatenate([jnp.where(lane < 64, x, zero), jnp.where(lane >= 64, x, zero)], axis=0).astype(jnp.bfloat16)

    def diagonal(x):
        return jnp.where(feat < 64, x[:, 0:128], x[:, 128:256])

    def forward(g):
        got(ymain(g))
        for i in range(2):
            both = jnp.concatenate([kv[g, n, 4:10, i].reshape(96, 128) for n in range(2)], axis=1)
            out = mm(packs[i], both, NN).astype(jnp.bfloat16)
            pack[g, i, 0, 48:128] = out[:, 0:128]
            pack[g, i, 1, 48:128] = out[:, 128:256]
        start(zcorner(g))

    def compute(gs):
        def all_rows(g, i):
            return jnp.concatenate([rim[g, 0, i], kv[g, i].reshape(320, 128), rim[g, 1, i]], axis=0)

        both = range(len(gs))
        qf = [cells(q_ref, g) * 0.125 for g in gs]
        uf = [cells(u_ref, g) for g in gs]
        s = [
            mm(
                jnp.concatenate([all_rows(gs[n], 0), kmask[...]], axis=1),
                jnp.concatenate([stacked(qf[n]), qmask[...]], axis=1),
                NT,
            )
            for n in both
        ]
        dp, pb, p, inv, ds = {}, {}, {}, {}, {}
        for n in both:
            p[n] = jnp.exp(s[n] - jnp.max(s[n], axis=0, keepdims=True))
            total = 1.0 / jnp.sum(p[n], axis=0, keepdims=True)
            inv[n] = jnp.where(feat < 64, total[:, 0:128], total[:, 128:256])
            pb[n] = p[n].astype(jnp.bfloat16)
            dp[n] = mm(all_rows(gs[n], 1), stacked(uf[n]), NT)
        for n in both:
            ot = diagonal(mm(all_rows(gs[n], 1), pb[n], TN)) * inv[n]
            put(o_ref, gs[n], ot.T)
            prod = uf[n].T * ot.astype(jnp.bfloat16).astype(jnp.float32)
            dots = jnp.concatenate(
                [jnp.sum(prod[0:64], axis=0, keepdims=True), jnp.sum(prod[64:128], axis=0, keepdims=True)], axis=1
            )
            ds[n] = (p[n] * (dp[n] - dots)).astype(jnp.bfloat16)
        for n in both:
            g = gs[n]
            turned = inv[n].T
            for i, grad in enumerate((mm(ds[n], stacked(qf[n] * turned), NN), mm(pb[n], stacked(uf[n] * turned), NN))):
                acc[g, i] = grad[128:448].reshape(10, 2, 16, 128)
                zs[g, 0, i] = grad[0:128].astype(jnp.bfloat16)
                zs[g, 1, i] = grad[448:576].astype(jnp.bfloat16)
        for g in gs:
            start(zgrad_corner(g))
        for g in gs:
            start(zgrad_own(g))
        for n, g in enumerate(gs):
            put(gq_ref, g, (diagonal(mm(all_rows(g, 0), ds[n], TN)) * (inv[n] * 0.125)).T)

    def unpack(g, which, rows, first, last):
        for side, block, have in ((0, 1, has_hi), (1, 0, has_lo)):
            @pl.when(have)
            def _(side=side, block=block):
                both = mm(which[block], jnp.concatenate([zr[g, side, 0, rows], zr[g, side, 1, rows]], axis=1), NN)
                for n in range(2):
                    part = both[:, 128 * n : 128 * n + 128].reshape(last - first, 16, 128)
                    acc[g, n, first:last, block] += part

    def stage_y(g):
        got(zgrad_corner(g))
        unpack(g, unpacks, corner_rows, 4, 10)
        ys[g, 0] = acc[g, :, 4:7].astype(jnp.bfloat16)
        ys[g, 1] = acc[g, :, 7:10].astype(jnp.bfloat16)
        start(ygrad(g))

    def stage_out(g):
        got(zgrad_own(g))
        unpack(g, unpacks_own, own_rows, 0, 4)
        got(ygrad(g))

        @pl.when(has_r)
        def _():
            acc[g, :, 1:4] += yr[g, 0].astype(jnp.float32)

        @pl.when(has_l)
        def _():
            acc[g, :, 0:3] += yr[g, 1].astype(jnp.float32)

        for i, ref in enumerate((gk_ref, gv_ref)):
            own = acc[g, i, 0:4].reshape(128, 128).astype(jnp.bfloat16)
            put(ref, g, mm(perm, own, TN))

    H = G // 2
    loads[2].wait()
    loads[3].wait()
    forward(0)
    forward(1)

    def step(h, carry):
        @pl.when(h + 1 < H)
        def _():
            forward(2 * h + 2)
            forward(2 * h + 3)

        @pl.when(h < H)
        def _():
            for g in (2 * h, 2 * h + 1):
                got(zown(g))
                got(zcorner(g))
            compute((2 * h, 2 * h + 1))

        @pl.when((h >= 1) & (h < H + 1))
        def _():
            stage_y(2 * h - 2)
            stage_y(2 * h - 1)

        @pl.when(h >= 2)
        def _():
            stage_out(2 * h - 4)
            stage_out(2 * h - 3)

        return carry

    lax.fori_loop(0, H + 2, step, 0)

    def drain(g, carry):
        for copies in (ymain(g), zown(g), zcorner(g), zgrad_own(g), zgrad_corner(g), ygrad(g)):
            sent(copies)
        return carry

    lax.fori_loop(0, G, drain, 0)


def on_device(queries, key_field, value_field, upstream):
    shape = queries.shape
    pairs = shape[3] // 128
    vmem = pl.BlockSpec(memory_space=pltpu.VMEM)
    hbm = pl.BlockSpec(memory_space=pltpu.HBM)
    dma = lambda: pltpu.SemaphoreType.DMA((pairs, 2))
    outs = pl.pallas_call(
        functools.partial(kernel, lax.axis_size("space"), lax.axis_size("tp")),
        out_shape=[jax.ShapeDtypeStruct(shape, jnp.bfloat16)] * 4,
        in_specs=[hbm] * 4,
        out_specs=[vmem] * 4,
        scratch_shapes=[pltpu.VMEM(shape, jnp.bfloat16) for _ in range(4)] + [
            pltpu.VMEM((pairs, 2, 10, 2, 16, 128), jnp.bfloat16),
            pltpu.VMEM((pairs, 2, 2, 128, 128), jnp.bfloat16),
            pltpu.VMEM((pairs, 2, 2, 128, 128), jnp.bfloat16),
            pltpu.VMEM((576, 128), jnp.bfloat16),
            pltpu.VMEM((256, 128), jnp.bfloat16),
            pltpu.VMEM((pairs, 2, 10, 2, 16, 128), jnp.float32),
            pltpu.VMEM((pairs, 2, 2, 128, 128), jnp.bfloat16),
            pltpu.VMEM((pairs, 2, 2, 128, 128), jnp.bfloat16),
            pltpu.VMEM((pairs, 2, 2, 3, 2, 16, 128), jnp.bfloat16),
            pltpu.VMEM((pairs, 2, 2, 3, 2, 16, 128), jnp.bfloat16),
        ] + [dma() for _ in range(12)] + [pltpu.SemaphoreType.DMA((4,))],
        compiler_params=pltpu.CompilerParams(
            collective_id=0, has_side_effects=True
        ),
        cost_estimate=pl.CostEstimate(flops=2 * 10**9, bytes_accessed=4 * 10**6, transcendentals=10**6),
        name="window_attention",
    )(queries, key_field, value_field, upstream)
    return tuple(outs)


def solution(mesh):
    spec = P("space", "tp", None, None)
    return jax.shard_map(
        on_device, mesh=mesh, in_specs=(spec,) * 4, out_specs=(spec,) * 4, check_vma=False
    )
```

time: 47.2 us -> 42.4 us (0.90)
  the two profiles are of different devices: /device:TPU:3 before, /device:TPU:1 now
where the time goes in v3:
time: 42.4 us; the launch traced here: 42.1 us
  Pallas kernels  36.9 us (87%)
  local copies, waits for them, and re-layouts  4.58 us (11%)
  between operations  0.65 us (2%)
    pallas_call x1, Pallas kernels, on_device(): pl.pallas_call(functools.partial(kernel, lax.axis_size('space'), lax.axis...  36.9 us
    unnamed x10, local copies, waits for them, and re-layouts  4.58 us

profile of v3, /device:TPU:1, one launch (start us, length us, event | category | flops | bytes accessed | tf_op | source)
XLA Modules:
  0.0 42.1 jit_solution(15422075345866662686)
XLA Ops:
  0.6 36.9 %window_attention.1 = (bf16[8,4,4,1024]{3,2,1,0:T(4,128)(2,1)}, bf16[8,4,4,1024]{3,2,1,0:T(4,128)(2,1)}, bf16[8,4,4,1024]{3,2,1,0:T(4,128)(2,1)}, bf16[8,4,4,1024]{3,2,1,0:T(4,128)(2,1)}) custom-call(bf16[8,4,4,1024]{3,2,1,0:T(4,128)(2,1)} %q_hbm.1, bf16[8,4,4,1024]{3,2,1,0:T(4,128)(2,1)} %k_hbm.1, bf16[8,4,4,1024]{3,2,1,0:T(4,128)(2,1)} %v_hbm.1, ...), custom_call_target="tpu_custom_call" | custom-call | flops 2000000000 | bytes 4000000 | tf_op jit(solution)/shard_map/window_attention/pallas_call | solution.py:342
  37.5 0.0 copy-start.2
  37.6 1.8 %copy.12 = bf16[8,4,4,1024]{3,2,1,0:T(4,128)(2,1)} copy(bf16[8,4,4,1024]{3,2,1,0:T(4,128)(2,1)} %get-tuple-element.8) | data formatting | bytes 524288
  39.3 0.0 copy-done.2
  39.4 0.0 copy-start.1
  39.4 0.7 %copy.13 = bf16[8,4,4,1024]{3,2,1,0:T(4,128)(2,1)} copy(bf16[8,4,4,1024]{3,2,1,0:T(4,128)(2,1)S(1)} %copy-done.2) | data formatting | bytes 524288
  40.1 0.3 copy-done.1
  40.4 0.0 copy-start
  40.4 0.7 %copy.14 = bf16[8,4,4,1024]{3,2,1,0:T(4,128)(2,1)} copy(bf16[8,4,4,1024]{3,2,1,0:T(4,128)(2,1)S(1)} %copy-done.1) | data formatting | bytes 524288
  41.1 0.3 copy-done
  41.4 0.7 %copy.15 = bf16[8,4,4,1024]{3,2,1,0:T(4,128)(2,1)} copy(bf16[8,4,4,1024]{3,2,1,0:T(4,128)(2,1)S(1)} %copy-done) | data formatting | bytes 524288
Async XLA Ops:
  37.5 1.8 %copy-start.2 = (bf16[8,4,4,1024]{3,2,1,0:T(4,128)(2,1)S(1)}, bf16[8,4,4,1024]{3,2,1,0:T(4,128)(2,1)}, u32[]{:S(2)}) copy-start(bf16[8,4,4,1024]{3,2,1,0:T(4,128)(2,1)} %get-tuple-element.9) | copy-start | bytes 786436
  39.4 1.0 %copy-start.1 = (bf16[8,4,4,1024]{3,2,1,0:T(4,128)(2,1)S(1)}, bf16[8,4,4,1024]{3,2,1,0:T(4,128)(2,1)}, u32[]{:S(2)}) copy-start(bf16[8,4,4,1024]{3,2,1,0:T(4,128)(2,1)} %get-tuple-element.10) | copy-start | bytes 786436
  40.4 1.0 %copy-start = (bf16[8,4,4,1024]{3,2,1,0:T(4,128)(2,1)S(1)}, bf16[8,4,4,1024]{3,2,1,0:T(4,128)(2,1)}, u32[]{:S(2)}) copy-start(bf16[8,4,4,1024]{3,2,1,0:T(4,128)(2,1)} %get-tuple-element.11) | copy-start | bytes 786436
